TPU v7x, 256 devices: a whole 4x4x8 slice. The times are simulated.
256 devices in a mesh: ctx: 32 (over z, x), dp: 8 (over y, core).
Axes of the slice: x: 4, y: 4, z: 8, core: 2. Of those that a mesh axis runs over, the one named last changes fastest.
Arguments:
- mel_frames: bfloat16 [8, 4096, 128], P('dp', 'ctx'), may hold values from -6 to 6
- conv_weight: bfloat16 [384, 1280], replicated, may hold values from -0.3125 to 0.3125
- conv_bias: float32 [1280], replicated, may hold values from -3 to 3
- video_hidden: bfloat16 [8, 4096, 5120], P('dp', 'ctx'), may hold values from -6 to 6
- video_count: int32 [8, 32], P('dp', 'ctx'), may hold values from 0 to 128, as said below
- video_places: int32 [8, 4096], P('dp', 'ctx'), may hold values from 0 to 6143, as said below
- audio_places: int32 [8, 4096], P('dp', 'ctx'), may hold values from 0 to 6143, as said below
- cotangent: bfloat16 [8, 6144, 3584], P('dp', 'ctx'), may hold values from -0.049804688 to 0.049804688
Outputs:
- grad_merger: float32 [32, 640, 896], P('ctx', 'dp')
- grad_audio: float32 [32, 160, 896], P('ctx', 'dp')
Inputs may be any that keep to these rules, and one draw needn't show every extreme that they name: `video_count`: in every sequence, shards 2i and 2i + 1 of encoder time hold 128 live video rows together, and some shard holds 128. `video_places`: in each sequence the live video slots (slot index within its shard below the shard's count) and the audio rows name every position exactly once; slots at or past the count hold arbitrary positions. `audio_places`: see video_places.
All inputs are finite; a program needn't handle non-finite values.
Results may differ from a plain program's by a relative error of at most 0.0029.
Values may be sent and summed in bfloat16 or wider, within the bound.
A program may use at most 128 MiB of HBM per device.

v0:
```python
import jax
import jax.numpy as jnp
from jax import lax
from jax.sharding import PartitionSpec as P

GRID_ROWS = 8


def partner(value, axis, stride):
    mask = 2**stride
    pairs = [(source, source ^ mask) for source in range(lax.axis_size(axis))]
    return lax.ppermute(value, axis, pairs)


def with_halo(cells, sides, width):
    for axis, dim in sides:
        count = lax.axis_size(axis)
        ends = count - 1
        head = lax.slice_in_dim(cells, 0, width, axis=dim)
        tail = lax.slice_in_dim(cells, cells.shape[dim] - width, cells.shape[dim], axis=dim)
        cells = jnp.concatenate(
            [
                lax.ppermute(tail, axis, [(i, (i + 1) % count) for i in range(ends)]),
                cells,
                lax.ppermute(head, axis, [((i + 1) % count, i) for i in range(ends)]),
            ],
            axis=dim,
        )
    return cells


def in_blocks(x, dim, devices):
    shape = x.shape
    tiles = x.reshape(*shape[:dim], devices, shape[dim] // devices, *shape[dim + 1 :])
    return jnp.moveaxis(tiles, dim, 0)


def sum_together(arrays, axis, dims):
    devices = lax.axis_size(axis)
    tiles = [in_blocks(a, dim, devices) for a, dim in zip(arrays, dims)]
    lines = jnp.concatenate([b.reshape(devices, -1) for b in tiles], axis=1)
    span = max(16, -(-lines.shape[1] // 1024) * 8)
    lines = jnp.pad(lines, ((0, 0), (0, span * 128 - lines.shape[1]))).reshape(-1, 128)
    flat, at, finished = (lax.psum_scatter(lines, axis, tiled=True).reshape(-1), 0, [])
    for b in tiles:
        part = b[0]
        finished.append(flat[at : at + part.size].reshape(part.shape))
        at += part.size
    return tuple(finished)


def frame_windows(padded):
    return jnp.concatenate([padded[:-2], padded[1:-1], padded[2:]], axis=1)


def spread_rows(values, block_width, copies):
    shaped = values.reshape(values.shape[0], GRID_ROWS, block_width)
    stacked = jnp.repeat(jnp.transpose(shaped, (1, 0, 2)), copies, axis=0)
    return stacked.reshape(-1, block_width)


def spread_columns(values, grid_cols, block_width):
    shaped = values.reshape(values.shape[0], grid_cols, block_width)
    stacked = jnp.tile(jnp.transpose(shaped, (1, 0, 2)), (GRID_ROWS, 1, 1))
    return stacked.reshape(-1, block_width)


def local(
    mel_frames,
    conv_weight,
    conv_bias,
    video_hidden,
    video_count,
    video_places,
    audio_places,
    cotangent,
):
    shards = lax.axis_size("ctx")
    grid_cols = shards // GRID_ROWS
    frames = mel_frames[0]
    hidden = video_hidden[0]
    places = video_places[0]
    audio_spots = audio_places[0]
    upstream = cotangent[0]
    block_rows = hidden.shape[1] // GRID_ROWS
    enc_rows = conv_weight.shape[1] // GRID_ROWS
    block_cols = upstream.shape[1] // grid_cols
    slot_ids = jnp.arange(hidden.shape[0], dtype=jnp.int32)
    live_count = video_count[0, 0]
    middle = hidden.shape[0] // 2
    got_rows, got_places = partner((hidden[middle:], places[middle:]), "ctx", 0)
    joined = jnp.concatenate([hidden[:middle], got_rows], axis=0)
    joined_places = jnp.concatenate([places[:middle], got_places], axis=0)
    lower_ids = slot_ids[:middle]
    source = jnp.where(
        (lower_ids < live_count) | (live_count >= middle),
        lower_ids,
        middle + lower_ids - live_count,
    )
    video_rows = jnp.take(joined, source, axis=0)
    video_spots = jnp.take(joined_places, source, axis=0)
    video_send = spread_rows(video_rows, block_rows, grid_cols)
    place_send = jnp.tile(video_spots, shards)
    upstream_send = spread_columns(upstream, grid_cols, block_cols)
    padded = with_halo(frames, (("ctx", 0),), 1)
    windows = frame_windows(padded)
    conv_out = jnp.dot(windows, conv_weight, preferred_element_type=jnp.float32) + conv_bias
    audio_hidden = jax.nn.gelu(conv_out, approximate=False).astype(jnp.bfloat16)
    audio_send = spread_rows(audio_hidden, enc_rows, grid_cols)
    got_video, got_places, got_upstream, got_audio, got_audio_spots = (
        lax.all_to_all(video_send, "ctx", split_axis=0, concat_axis=0, tiled=True),
        lax.all_to_all(place_send, "ctx", split_axis=0, concat_axis=0, tiled=True),
        lax.all_to_all(upstream_send, "ctx", split_axis=0, concat_axis=0, tiled=True),
        lax.all_to_all(audio_send, "ctx", split_axis=0, concat_axis=0, tiled=True),
        lax.all_to_all(
            jnp.tile(audio_spots, shards), "ctx", split_axis=0, concat_axis=0, tiled=True
        ),
    )
    picked = jnp.take(got_upstream, jnp.maximum(got_places, 0), axis=0)
    picked = jnp.where((got_places >= 0)[:, None], picked, jnp.zeros_like(picked))
    contract = (((0,), (0,)), ((), ()))
    merger_block = lax.dot_general(got_video, picked, contract, preferred_element_type=jnp.float32)
    audio_picked = jnp.take(got_upstream, got_audio_spots, axis=0)
    audio_block = lax.dot_general(
        got_audio, audio_picked, contract, preferred_element_type=jnp.float32
    )
    merger_part, audio_part = sum_together((merger_block, audio_block), "dp", (0, 0))
    return (merger_part[None], audio_part[None])


def solution(mesh):
    return jax.shard_map(
        local,
        mesh=mesh,
        in_specs=(
            P("dp", "ctx", None),
            P(),
            P(),
            P("dp", "ctx", None),
            P("dp", "ctx"),
            P("dp", "ctx"),
            P("dp", "ctx"),
            P("dp", "ctx", None),
        ),
        out_specs=(P("ctx", "dp", None), P("ctx", "dp", None)),
        check_vma=False,
    )
```

profile of v0, /device:TPU:6, one launch (start us, length us, event | category | flops | bytes accessed | tf_op | source)
XLA Modules:
  0.0 470.8 jit_solution(9093201872016080622)
XLA Ops:
  7.2 0.8 slice_bitcast_fusion.5
  8.0 0.8 collective-permute-start.1
  9.5 2.0 collective-permute-done.1
  11.6 0.8 gather_fusion.1
  12.4 0.6 all_to_all.41
  13.0 11.6 %all-to-all-start.1 = ((s32[32,64,1]{1,2,0:T(1,128)}), s32[32,64,1]{1,2,0:T(1,128)S(1)}, u32[]{:S(2)}, u32[]{:S(2)}) async-start(s32[32,64,1]{1,2,0:T(1,128)} %all_to_all.41), calls=%async_computation.1 | async-start | bytes 32768 | tf_op jit(solution)/shard_map/all_to_all | solution.py:112
  24.6 0.7 slice_bitcast_fusion.3
  25.3 2.8 collective-permute-start.3
  28.1 5.2 %collective-permute-start.2 = (bf16[1,128]{1,0:T(2,128)(2,1)S(1)}, bf16[1,128]{1,0:T(2,128)(2,1)S(1)}, u32[]{:S(2)}, u32[]{:S(2)}) collective-permute-start(bf16[1,128]{1,0:T(2,128)(2,1)S(1)} %get-tuple-element.8), channel_id=1, source_target_pairs={{0,8},{8,16},{16,24},{24,32},{32,40},{40,48},{48,56},{56,64},{64,7... | collective-permute-start | bytes 776 | tf_op jit(solution)/shard_map/ppermute | solution.py:23
  33.3 1.3 all_to_all.48
  34.5 9.5 %all-to-all-start.4 = ((s32[32,128,1]{1,2,0:T(1,128)}), s32[32,128,1]{1,2,0:T(1,128)S(1)}, u32[]{:S(2)}, u32[]{:S(2)}) async-start(s32[32,128,1]{1,2,0:T(1,128)} %all_to_all.48), calls=%async_computation.4 | async-start | bytes 32768 | tf_op jit(solution)/shard_map/all_to_all | solution.py:115
  44.1 2.5 fusion.15
  46.5 0.2 copy.22
  46.7 5.2 %all-to-all-done.4 = s32[32,128,1]{1,2,0:T(1,128)S(1)} async-done(((s32[32,128,1]{1,2,0:T(1,128)}), s32[32,128,1]{1,2,0:T(1,128)S(1)}, u32[]{:S(2)}, u32[]{:S(2)}) %all-to-all-start.4) | async-done | bytes 16416 | tf_op jit(solution)/shard_map/all_to_all | solution.py:115
  51.9 1.3 broadcast_in_dim.66
  53.2 6.3 %all-to-all-start.3 = ((bf16[32,128,160]{1,2,0:T(8,128)(2,1)}), bf16[32,128,160]{1,2,0:T(8,128)(2,1)}, u32[]{:S(2)}, u32[]{:S(2)}) async-start(bf16[32,128,160]{1,2,0:T(8,128)(2,1)} %bitcast.16), calls=%async_computation.3 | async-start | bytes 2621440 | tf_op jit(solution)/shard_map/all_to_all | solution.py:114
  59.5 1.3 reshape_squeeze.3
  60.8 1.5 copy.21
  62.3 27.6 %all-to-all-done.3 = bf16[32,128,160]{1,2,0:T(8,128)(2,1)} async-done(((bf16[32,128,160]{1,2,0:T(8,128)(2,1)}), bf16[32,128,160]{1,2,0:T(8,128)(2,1)}, u32[]{:S(2)}, u32[]{:S(2)}) %all-to-all-start.3) | async-done | bytes 1310752 | tf_op jit(solution)/shard_map/all_to_all | solution.py:114
  89.9 5.6 %tile.6 = bf16[8,4,192,896]{3,2,1,0:T(8,128)(2,1)} broadcast(bf16[4,192,896]{2,1,0:T(8,128)(2,1)S(1)} %copy.21), dimensions={1,2,3} | broadcast | bytes 12386304 | tf_op jit(solution)/shard_map/tile | solution.py:64
  95.5 5.7 %all-to-all-start.2 = ((bf16[32,192,896]{2,1,0:T(8,128)(2,1)}), bf16[32,192,896]{2,1,0:T(8,128)(2,1)}, u32[]{:S(2)}, u32[]{:S(2)}) async-start(bf16[32,192,896]{2,1,0:T(8,128)(2,1)} %bitcast.43), calls=%async_computation.2 | async-start | bytes 22020096 | tf_op jit(solution)/shard_map/all_to_all | solution.py:113
  101.3 0.1 slice_bitcast_fusion.1
  101.4 0.9 collective-permute-start
  102.3 63.4 %collective-permute-done = bf16[64,5120]{1,0:T(8,128)(2,1)S(1)} collective-permute-done((bf16[64,5120]{1,0:T(8,128)(2,1)S(1)}, bf16[64,5120]{1,0:T(8,128)(2,1)S(1)}, u32[]{:S(2)}, u32[]{:S(2)}) %collective-permute-start) | collective-permute-done | bytes 655392 | tf_op jit(solution)/shard_map/ppermute | solution.py:12
  165.7 0.1 pad_maximum_fusion
  165.8 0.9 gather_fusion
  166.8 0.2 bitcast_select_fusion
  167.1 168.7 %all-to-all-done.2 = bf16[32,192,896]{2,1,0:T(8,128)(2,1)} async-done(((bf16[32,192,896]{2,1,0:T(8,128)(2,1)}), bf16[32,192,896]{2,1,0:T(8,128)(2,1)}, u32[]{:S(2)}, u32[]{:S(2)}) %all-to-all-start.2) | async-done | bytes 11010080 | tf_op jit(solution)/shard_map/all_to_all | solution.py:113
  335.8 1.9 broadcast_in_dim.60
  337.7 11.2 %all-to-all-start = ((bf16[32,64,640]{2,1,0:T(8,128)(2,1)}), bf16[32,64,640]{2,1,0:T(8,128)(2,1)}, u32[]{:S(2)}, u32[]{:S(2)}) async-start(bf16[32,64,640]{2,1,0:T(8,128)(2,1)} %bitcast.44), calls=%async_computation | async-start | bytes 5242880 | tf_op jit(solution)/shard_map/all_to_all | solution.py:111
  348.9 0.2 reduce-scatter.2.cloned.1.call-start
  349.3 0.1 compare_reduce_fusion.1
  349.4 0.1 le.42
  349.5 0.1 ge.43
  349.6 25.3 %gather_fusion.3 = bf16[4096,896]{1,0:T(8,128)(2,1)} fusion(bf16[6144,896]{1,0:T(8,128)(2,1)} %bitcast.10, s32[4096]{0:T(1024)S(1)} %broadcast_clamp_fusion), kind=kCustom, calls=%fused_computation.3 | custom fusion | bytes 14696448 | tf_op jit(solution)/shard_map/jit(_take)/gather | solution.py:123
  375.0 5.4 %fusion = f32[160,896]{1,0:T(8,128)S(1)} fusion(bf16[4096,896]{1,0:T(8,128)(2,1)} %gather_fusion.3, pred[4096]{0:T(1024)(128)(4,1)S(1)} %compare_and_fusion, bf16[32,128,160]{1,2,0:T(8,128)(2,1)} %all-to-all-done.3), kind=kOutput, calls=%fused_computation.4 | convolution fusion | flops 1178075136 | bytes 9228288 | tf_op jit(solution)/shard_map/dot_general | solution.py:124
  380.3 1.0 reshape_reshape.9
  381.3 16.0 %gather_fusion.2 = bf16[2048,896]{1,0:T(8,128)(2,1)} fusion(bf16[6144,896]{1,0:T(8,128)(2,1)} %bitcast.10, s32[2048]{0:T(1024)S(1)} %broadcast_clamp_fusion.1), kind=kCustom, calls=%fused_computation.2 | custom fusion | bytes 7348224 | tf_op jit(solution)/shard_map/jit(_take)/gather | solution.py:119
  397.2 12.6 %all-to-all-done = bf16[32,64,640]{2,1,0:T(8,128)(2,1)} async-done(((bf16[32,64,640]{2,1,0:T(8,128)(2,1)}), bf16[32,64,640]{2,1,0:T(8,128)(2,1)}, u32[]{:S(2)}, u32[]{:S(2)}) %all-to-all-start) | async-done | bytes 2621472 | tf_op jit(solution)/shard_map/all_to_all | solution.py:111
  409.8 7.3 %fusion.4 = f32[640,896]{1,0:T(8,128)} fusion(bf16[2048,640]{1,0:T(8,128)(2,1)} %bitcast.5, bf16[2048,896]{1,0:T(8,128)(2,1)} %gather_fusion.2, pred[2048]{0:T(1024)(128)(4,1)S(1)} %le.42, pred[2048]{0:T(1024)(128)(4,1)S(1)} %ge.43), kind=kOutput, calls=%fused_computation.8 | convolution fusion | flops 2352480256 | bytes 8589312 | tf_op jit(solution)/shard_map/dot_general | solution.py:122
  417.1 2.0 reshape_reshape.8
  419.1 2.8 select_maximum_fusion
  421.9 3.8 reshape.123
  425.8 34.8 %reduce-scatter.2.cloned.1.call-done = f32[704,128]{1,0:T(8,128)} async-done(((f32[5632,128]{1,0:T(8,128)}), f32[704,128]{1,0:T(8,128)}) %reduce-scatter.2.cloned.1.call-update) | async-done | bytes 360464 | tf_op jit(solution)/shard_map/reduce_scatter | solution.py:44
  460.6 1.0 slice.84
  461.6 0.8 broadcast_in_dim_reshape.6
  462.3 0.9 slice.85
  463.2 0.7 broadcast_in_dim_reshape.7
  (23 shorter events, 0.5 us)
Async XLA Ops:
  7.2 36.9 %copy-start = (bf16[384,1280]{1,0:T(8,128)(2,1)S(1)}, bf16[384,1280]{1,0:T(8,128)(2,1)}, u32[]{:S(2)}) copy-start(bf16[384,1280]{1,0:T(8,128)(2,1)} %param.9) | copy-start | bytes 2949124
  8.0 3.5 collective-permute-start.1
  13.0 20.2 %all-to-all-start.1 = ((s32[32,64,1]{1,2,0:T(1,128)}), s32[32,64,1]{1,2,0:T(1,128)S(1)}, u32[]{:S(2)}, u32[]{:S(2)}) async-start(s32[32,64,1]{1,2,0:T(1,128)} %all_to_all.41), calls=%async_computation.1 | async-start | bytes 32768 | tf_op jit(solution)/shard_map/all_to_all | solution.py:112
  25.3 18.7 %collective-permute-start.3 = (bf16[1,128]{1,0:T(2,128)(2,1)S(1)}, bf16[1,128]{1,0:T(2,128)(2,1)S(1)}, u32[]{:S(2)}, u32[]{:S(2)}) collective-permute-start(bf16[1,128]{1,0:T(2,128)(2,1)S(1)} %get-tuple-element.9), channel_id=1, source_target_pairs={{8,0},{16,8},{24,16},{32,24},{40,32},{48,40},{56,48},{64,56},{72,6... | collective-permute-start | bytes 776 | tf_op jit(solution)/shard_map/ppermute | solution.py:25
  28.1 16.0 %collective-permute-start.2 = (bf16[1,128]{1,0:T(2,128)(2,1)S(1)}, bf16[1,128]{1,0:T(2,128)(2,1)S(1)}, u32[]{:S(2)}, u32[]{:S(2)}) collective-permute-start(bf16[1,128]{1,0:T(2,128)(2,1)S(1)} %get-tuple-element.8), channel_id=1, source_target_pairs={{0,8},{8,16},{16,24},{24,32},{32,40},{40,48},{48,56},{56,64},{64,7... | collective-permute-start | bytes 776 | tf_op jit(solution)/shard_map/ppermute | solution.py:23
  34.5 17.4 %all-to-all-start.4 = ((s32[32,128,1]{1,2,0:T(1,128)}), s32[32,128,1]{1,2,0:T(1,128)S(1)}, u32[]{:S(2)}, u32[]{:S(2)}) async-start(s32[32,128,1]{1,2,0:T(1,128)} %all_to_all.48), calls=%async_computation.4 | async-start | bytes 32768 | tf_op jit(solution)/shard_map/all_to_all | solution.py:115
  46.5 13.0 %copy-start.1 = (bf16[1,192,3584]{2,1,0:T(8,128)(2,1)S(1)}, bf16[1,192,3584]{2,1,0:T(8,128)(2,1)}, u32[]{:S(2)}) copy-start(bf16[1,192,3584]{2,1,0:T(8,128)(2,1)} %param.15) | copy-start | bytes 4128772
  53.2 36.7 %all-to-all-start.3 = ((bf16[32,128,160]{1,2,0:T(8,128)(2,1)}), bf16[32,128,160]{1,2,0:T(8,128)(2,1)}, u32[]{:S(2)}, u32[]{:S(2)}) async-start(bf16[32,128,160]{1,2,0:T(8,128)(2,1)} %bitcast.16), calls=%async_computation.3 | async-start | bytes 2621440 | tf_op jit(solution)/shard_map/all_to_all | solution.py:114
  95.5 5.8 %copy-start.2 = (bf16[1,128,5120]{2,1,0:T(8,128)(2,1)S(1)}, bf16[1,128,5120]{2,1,0:T(8,128)(2,1)}, u32[]{:S(2)}) copy-start(bf16[1,128,5120]{2,1,0:T(8,128)(2,1)} %param.11) | copy-start | bytes 3932164
  95.5 240.3 %all-to-all-start.2 = ((bf16[32,192,896]{2,1,0:T(8,128)(2,1)}), bf16[32,192,896]{2,1,0:T(8,128)(2,1)}, u32[]{:S(2)}, u32[]{:S(2)}) async-start(bf16[32,192,896]{2,1,0:T(8,128)(2,1)} %bitcast.43), calls=%async_computation.2 | async-start | bytes 22020096 | tf_op jit(solution)/shard_map/all_to_all | solution.py:113
  101.4 64.4 %collective-permute-start = (bf16[64,5120]{1,0:T(8,128)(2,1)S(1)}, bf16[64,5120]{1,0:T(8,128)(2,1)S(1)}, u32[]{:S(2)}, u32[]{:S(2)}) collective-permute-start(bf16[64,5120]{1,0:T(8,128)(2,1)S(1)} %get-tuple-element.7), channel_id=1, source_target_pairs={{0,8},{8,0},{16,24},{24,16},{32,40},{40,32},{48,56},{56,48},{64,72... | collective-permute-start | bytes 1966088 | tf_op jit(solution)/shard_map/ppermute | solution.py:12
  337.7 72.1 %all-to-all-start = ((bf16[32,64,640]{2,1,0:T(8,128)(2,1)}), bf16[32,64,640]{2,1,0:T(8,128)(2,1)}, u32[]{:S(2)}, u32[]{:S(2)}) async-start(bf16[32,64,640]{2,1,0:T(8,128)(2,1)} %bitcast.44), calls=%async_computation | async-start | bytes 5242880 | tf_op jit(solution)/shard_map/all_to_all | solution.py:111
  348.9 111.7 %reduce-scatter.2.cloned.1.call-start = ((), (), s32[]{:S(2)}) async-start(), calls=%async_computation.6 | async-start | bytes 3244032 | tf_op jit(solution)/shard_map/reduce_scatter | solution.py:44
Sparse Core Ops, SparseCore 0:
  425.9 34.6 reduce-scatter.1
where the time goes:
time: 472 us; the launch traced here: 471 us
  waiting for transfers between devices  314 us (67%)
  local copies, waits for them, and re-layouts  68.8 us (15%)
  starting transfers between devices  54.2 us (11%)
  matrix products  15.1 us (3%)
  between operations  14.9 us (3%)
    all_to_all x1, waiting for transfers between devices, local(): lax.all_to_all(upstream_send, 'ctx', split_axis=0, concat_axis=0, tiled=T...  169 us
    ppermute x2, waiting for transfers between devices, partner(): return lax.ppermute(value, axis, pairs)  65.5 us
    reduce_scatter x1, waiting for transfers between devices, sum_together(): lax.psum_scatter(lines, axis, tiled=True).reshape(-1)  34.8 us
    all_to_all x1, waiting for transfers between devices, local(): lax.all_to_all(audio_send, 'ctx', split_axis=0, concat_axis=0, tiled=True)  27.6 us
    gather x1, local copies, waits for them, and re-layouts, local(): audio_picked = jnp.take(got_upstream, got_audio_spots, axis=0)  25.3 us
    gather x1, local copies, waits for them, and re-layouts, local(): picked = jnp.take(got_upstream, jnp.maximum(got_places, 0), axis=0)  16 us
    all_to_all x1, waiting for transfers between devices, local(): lax.all_to_all(video_send, 'ctx', split_axis=0, concat_axis=0, tiled=True)  12.6 us
    all_to_all x1, starting transfers between devices, local(): lax.all_to_all(place_send, 'ctx', split_axis=0, concat_axis=0, tiled=True)  11.6 us
  transfers between devices with their start and end apart: 10, of which 7 were waited for; matrix products, arithmetic and copies ran while one was open for 12% of the time, Pallas kernels for 0%

commit v1 on v0

v1 whole, which is shorter than its diff:
```python
import jax
import jax.numpy as jnp
from jax import lax
from jax.sharding import Mesh, PartitionSpec as P

GRID_ROWS = 8
GRID_COLS = 4


def local(mel, conv_weight, conv_bias, video_hidden, video_count, video_places, audio_places, cotangent):
    z = lax.axis_index("z")
    hidden = video_hidden[0]
    places = video_places[0]
    upstream = cotangent[0]
    block_cols = upstream.shape[1] // GRID_COLS
    enc = conv_weight.shape[1] // GRID_ROWS

    cols = lax.all_to_all(
        jnp.transpose(upstream.reshape(-1, GRID_COLS, block_cols), (1, 0, 2)), "x", 0, 0, tiled=True
    )
    up = lax.all_gather(cols, "z", tiled=True).reshape(-1, block_cols)

    live_count = video_count[0, 0]
    middle = hidden.shape[0] // 2
    pairs = [(i, i ^ 1) for i in range(lax.axis_size("x"))]
    got_rows, got_places = lax.ppermute((hidden[middle:], places[middle:]), "x", pairs)
    joined = jnp.concatenate([hidden[:middle], got_rows], axis=0)
    joined_places = jnp.concatenate([places[:middle], got_places], axis=0)
    ids = jnp.arange(middle, dtype=jnp.int32)
    source = jnp.where((ids < live_count) | (live_count >= middle), ids, middle + ids - live_count)
    rows = jnp.take(joined, source, axis=0)
    spots = jnp.take(joined_places, source, axis=0)
    rows = lax.all_to_all(
        jnp.transpose(rows.reshape(middle, GRID_ROWS, -1), (1, 0, 2)), "z", 0, 0, tiled=True
    )
    rows = lax.all_gather(rows, "x", axis=1, tiled=False)
    rows = rows.reshape(-1, rows.shape[-1])
    spots = lax.all_gather(lax.all_gather(spots, "x"), "z").reshape(-1)

    frames = lax.all_gather(lax.all_gather(mel[0], "x"), "z").reshape(-1, mel.shape[-1])
    audio_spots = lax.all_gather(lax.all_gather(audio_places[0], "x"), "z").reshape(-1)
    pad = jnp.zeros((1, frames.shape[1]), frames.dtype)
    padded = jnp.concatenate([pad, frames, pad], axis=0)
    windows = jnp.concatenate([padded[:-2], padded[1:-1], padded[2:]], axis=1)
    weight = lax.dynamic_slice_in_dim(conv_weight, z * enc, enc, axis=1)
    bias = lax.dynamic_slice_in_dim(conv_bias, z * enc, enc, axis=0)
    conv = jnp.dot(windows, weight, preferred_element_type=jnp.float32) + bias
    audio = jax.nn.gelu(conv, approximate=False).astype(jnp.bfloat16)

    contract = (((0,), (0,)), ((), ()))
    merger = lax.dot_general(rows, jnp.take(up, spots, axis=0), contract, preferred_element_type=jnp.float32)
    audio_block = lax.dot_general(
        audio, jnp.take(up, audio_spots, axis=0), contract, preferred_element_type=jnp.float32
    )
    merger = lax.psum_scatter(merger, ("y", "core"), tiled=True)
    audio_block = lax.psum_scatter(
        audio_block.reshape(GRID_ROWS, enc // GRID_ROWS, block_cols), ("y", "core"), tiled=True
    )
    return merger[None], audio_block


def solution(mesh):
    whole = Mesh(mesh.devices.reshape(8, 4, 4, 2), ("z", "x", "y", "core"))
    dp, ctx = ("y", "core"), ("z", "x")
    return jax.shard_map(
        local,
        mesh=whole,
        in_specs=(
            P(dp, ctx, None),
            P(),
            P(),
            P(dp, ctx, None),
            P(dp, ctx),
            P(dp, ctx),
            P(dp, ctx),
            P(dp, ctx, None),
        ),
        out_specs=(P(ctx, dp, None), P(ctx, dp, None)),
        check_vma=False,
    )
```

time: 472 us -> 307 us (0.65)
  waiting for transfers between devices: 314 us -> 105 us
  blocking collectives: 0 us -> 95.6 us
  starting transfers between devices: 54.2 us -> 11.3 us
  local copies, waits for them, and re-layouts: 68.8 us -> 56.5 us
  matrix products: 15.1 us -> 20.4 us
    all_to_all x5 -> x1, waiting for transfers between devices: 214 us -> 0.01 us  [local(): lax.all_to_all(jnp.transpose(rows.reshape(middle, GRID_ROWS, -1), (1, 0,...]
    all_gather x0 -> x5, blocking collectives: none -> 77.1 us  [the longest x2 29.5 us: local(): spots = lax.all_gather(lax.all_gather(spots, 'x'), 'z').reshape(-1)]
    ppermute x4 -> x2, waiting for transfers between devices: 65.5 us -> 10.4 us  [local(): lax.ppermute((hidden[middle:], places[middle:]), 'x', pairs)]
    all_gather x0 -> x3, waiting for transfers between devices: none -> 48.1 us  [the longest x1 48.1 us: local(): up = lax.all_gather(cols, 'z', tiled=True).reshape(-1, block_cols)]
    all_to_all x5 -> x1, starting transfers between devices: 44.3 us -> 9.19 us  [local(): lax.all_to_all(jnp.transpose(rows.reshape(middle, GRID_ROWS, -1), (1, 0,...]
    all_to_all x0 -> x1, blocking collectives: none -> 18.5 us  [local(): lax.all_to_all(jnp.transpose(upstream.reshape(-1, GRID_COLS, block_cols),...]
    unnamed x1 -> x6, waiting for transfers between devices: 0.02 us -> 10 us
    another operation x6 -> x1, local copies, waits for them, and re-layouts: 11.3 us -> 2.76 us  [local(): upstream.reshape(-1, GRID_COLS, block_cols)]
  transfers between devices with their start and end apart: 10 -> 8, of which waited for: 7 -> 4; matrix products, arithmetic and copies ran while one was open for 12% -> 25% of each run, Pallas kernels for 0% -> 0%
where the time goes in v1:
time: 307 us; the launch traced here: 306 us
  waiting for transfers between devices  105 us (34%)
  blocking collectives  95.6 us (31%)
  local copies, waits for them, and re-layouts  56.5 us (18%)
  matrix products  20.4 us (7%)
  between operations  14.6 us (5%)
  starting transfers between devices  11.3 us (4%)
    all_gather x1, waiting for transfers between devices, local(): up = lax.all_gather(cols, 'z', tiled=True).reshape(-1, block_cols)  48.1 us
    reduce_scatter x1, waiting for transfers between devices, local(): merger = lax.psum_scatter(merger, ('y', 'core'), tiled=True)  36.8 us
    all_gather x2, blocking collectives, local(): spots = lax.all_gather(lax.all_gather(spots, 'x'), 'z').reshape(-1)  29.5 us
    all_gather x1, blocking collectives, local(): lax.all_gather(lax.all_gather(audio_places[0], 'x'), 'z').reshape(-1)  26.3 us
    gather x1, local copies, waits for them, and re-layouts, local(): jnp.take(up, audio_spots, axis=0)  25.4 us
    all_to_all x1, blocking collectives, local(): lax.all_to_all(jnp.transpose(upstream.reshape(-1, GRID_COLS, block_cols),...  18.5 us
    gather x1, local copies, waits for them, and re-layouts, local(): jnp.take(up, spots, axis=0)  16 us
    all_gather x1, blocking collectives, local(): lax.all_gather(mel[0], 'x')  13.4 us
  transfers between devices with their start and end apart: 8, of which 4 were waited for; matrix products, arithmetic and copies ran while one was open for 25% of the time, Pallas kernels for 0%

profile of v1, /device:TPU:6, one launch (start us, length us, event | category | flops | bytes accessed | tf_op | source)
XLA Modules:
  0.0 306.1 jit_solution(9559356676186818272)
XLA Ops:
  7.2 0.0 copy-start
  7.2 0.0 all-gather.16.cloned.1.call-start
  7.2 13.4 %all_gather.43 = bf16[4,128,128]{2,1,0:T(8,128)(2,1)} all-gather(bf16[1,128,128]{2,1,0:T(8,128)(2,1)} %param.8), channel_id=1, replica_groups=mesh['z'=8,'x'=4,'y'=4,'core'=2] {'x'}, dimensions={0}, use_global_device_ids=true | all-gather | bytes 163840 | tf_op jit(solution)/shard_map/all_gather | solution.py:40
  20.7 0.0 all-gather.16.cloned.1.call-update
  20.7 0.0 all-gather.12.cloned.1.call-start
  20.7 2.8 reshape_squeeze.3
  23.5 0.2 copy.21
  23.7 0.0 copy-start.2
  23.7 18.5 %all_to_all.10 = bf16[4,192,896]{2,1,0:T(8,128)(2,1)} all-to-all(bf16[4,192,896]{2,1,0:T(8,128)(2,1)S(1)} %copy.21), channel_id=1, replica_groups=mesh['z'=8,'x'=4,'y'=4,'core'=2] {'x'}, dimensions={0} | all-to-all | bytes 2752512 | tf_op jit(solution)/shard_map/all_to_all | solution.py:18
  42.2 0.0 all-gather.12.cloned.1.call-update
  42.2 1.0 slice_bitcast_fusion.1
  43.2 1.2 collective-permute-start
  45.1 10.4 %collective-permute-done = bf16[64,5120]{1,0:T(8,128)(2,1)S(1)} collective-permute-done((bf16[64,5120]{1,0:T(8,128)(2,1)}, bf16[64,5120]{1,0:T(8,128)(2,1)S(1)}, u32[]{:S(2)}, u32[]{:S(2)}) %collective-permute-start) | collective-permute-done | bytes 655392 | tf_op jit(solution)/shard_map/ppermute | solution.py:26
  55.5 0.9 copy-done.4
  56.4 1.2 pad_maximum_fusion
  57.6 0.9 gather_fusion
  58.5 0.0 copy-start.5
  58.5 0.0 copy-start.6
  58.6 1.0 fusion.58
  59.6 9.2 %all-to-all-start = ((bf16[8,64,640]{2,1,0:T(8,128)(2,1)}), bf16[8,64,640]{2,1,0:T(8,128)(2,1)S(1)}, u32[]{:S(2)}, u32[]{:S(2)}) async-start(bf16[8,64,640]{2,1,0:T(8,128)(2,1)} %fusion.58), calls=%async_computation | async-start | bytes 1310720 | tf_op jit(solution)/shard_map/all_to_all | solution.py:33
  68.8 0.0 all-gather.14.cloned.1.call-start
  68.8 0.1 slice_bitcast_fusion.3
  68.9 0.5 collective-permute-start.1
  69.4 7.9 %all-gather.6 = s32[4,1,128]{2,1,0:T(1,128)S(1)} all-gather(s32[1,1,128]{2,1,0:T(1,128)S(1)} %bitcast.54), channel_id=1, replica_groups=mesh['z'=8,'x'=4,'y'=4,'core'=2] {'x'}, dimensions={0}, use_global_device_ids=true | all-gather | bytes 2560 | tf_op jit(solution)/shard_map/all_gather | solution.py:41
  77.3 26.3 %all-gather.7 = s32[8,4,128]{2,1,0:T(4,128)S(1)} all-gather(s32[1,4,128]{2,1,0:T(4,128)S(1)} %bitcast.53), channel_id=5, replica_groups=mesh['z'=8,'x'=4,'y'=4,'core'=2] {'z'}, dimensions={0}, use_global_device_ids=true | all-gather | bytes 18432 | tf_op jit(solution)/shard_map/all_gather | solution.py:41
  103.6 0.9 copy-done.1
  104.4 0.0 all-gather.14.cloned.1.call-update
  104.4 0.0 reduce-scatter.7.cloned.1.call-start
  104.6 0.8 dynamic_slice.7
  105.3 0.1 pad_add_fusion
  105.4 0.8 gather_fusion.1
  106.2 8.2 %all-gather.4 = s32[4,1,64]{2,1,0:T(1,128)S(1)} all-gather(s32[1,1,64]{2,1,0:T(1,128)S(1)} %fusion.62), channel_id=1, replica_groups=mesh['z'=8,'x'=4,'y'=4,'core'=2] {'x'}, dimensions={0}, use_global_device_ids=true | all-gather | bytes 1280 | tf_op jit(solution)/shard_map/all_gather | solution.py:38
  114.4 21.3 %all-gather.5 = s32[8,4,64]{2,1,0:T(4,128)S(1)} all-gather(s32[1,4,64]{2,1,0:T(4,128)S(1)} %bitcast.52), channel_id=3, replica_groups=mesh['z'=8,'x'=4,'y'=4,'core'=2] {'z'}, dimensions={0}, use_global_device_ids=true | all-gather | bytes 9216 | tf_op jit(solution)/shard_map/all_gather | solution.py:38
  135.7 0.1 reshape.197
  135.8 3.1 %pad_slice_fusion.1 = (bf16[4096,128]{1,0:T(8,128)(2,1)S(1)}, bf16[4096,128]{1,0:T(8,128)(2,1)}) fusion(bf16[4096,128]{1,0:T(8,128)(2,1)} %bitcast.46), kind=kLoop, calls=%fused_computation.69 | loop fusion | bytes 3145728 | tf_op jit(solution)/shard_map/slice | solution.py:44
  138.9 48.1 %all-gather.12.cloned.1.call-done = bf16[32,192,896]{2,1,0:T(8,128)(2,1)} async-done(((bf16[4,192,896]{2,1,0:T(8,128)(2,1)}), bf16[32,192,896]{2,1,0:T(8,128)(2,1)}) %all-gather.12.cloned.1.call-update) | async-done | bytes 11010064 | tf_op jit(solution)/shard_map/all_gather | solution.py:21
  187.0 25.4 %gather_fusion.3 = bf16[4096,896]{1,0:T(8,128)(2,1)} fusion(bf16[6144,896]{1,0:T(8,128)(2,1)} %bitcast.42, s32[4096]{0:T(1024)S(1)} %broadcast_clamp_fusion), kind=kCustom, calls=%fused_computation.3 | custom fusion | bytes 14696448 | tf_op jit(solution)/shard_map/jit(_take)/gather | solution.py:53
  212.5 13.2 %fusion = f32[160,896]{1,0:T(8,128)} fusion(bf16[4096,896]{1,0:T(8,128)(2,1)} %gather_fusion.3, pred[4096]{0:T(1024)(128)(4,1)S(1)} %compare_and_fusion, bf16[4096,128]{1,0:T(8,128)(2,1)} %get-tuple-element.13, bf16[4096,128]{1,0:T(8,128)(2,1)S(1)} %bitcast.47, bf16[4096,128]{1,0:T(8,128)(2,1)S(1)} %get-tuple-element.12, f32[160]{0:T(256)S(1)} %dynamic_slice.7, ...), kind=kOutput, calls=%fused_computation.4 | convolution fusion | flops 1734082560 | bytes 11260932 | tf_op jit(solution)/shard_map/dot_general | solution.py:52
  225.6 2.0 reshape.201
  227.6 0.0 reduce-scatter.7.cloned.1.call-update
  227.6 0.3 reduce-scatter.5.cloned.1.call-start
  227.9 0.1 reshape.195
  228.0 16.0 %gather_fusion.2 = bf16[2048,896]{1,0:T(8,128)(2,1)} fusion(bf16[6144,896]{1,0:T(8,128)(2,1)} %bitcast.43, s32[2048]{0:T(1024)S(1)} %broadcast_clamp_fusion.1), kind=kCustom, calls=%fused_computation.2 | custom fusion | bytes 7348224 | tf_op jit(solution)/shard_map/jit(_take)/gather | solution.py:51
  244.0 7.2 %fusion.4 = f32[640,896]{1,0:T(8,128)} fusion(bf16[2048,640]{1,0:T(8,128)(2,1)} %bitcast.55, bf16[2048,896]{1,0:T(8,128)(2,1)} %gather_fusion.2, pred[2048]{0:T(1024)(128)(4,1)S(1)} %compare_and_fusion.1), kind=kOutput, calls=%fused_computation.10 | convolution fusion | flops 2350645248 | bytes 8587264 | tf_op jit(solution)/shard_map/dot_general | solution.py:51
  251.2 0.0 reduce-scatter.5.cloned.1.call-update
  251.2 9.9 %reduce-scatter.7.cloned.1.call-done = f32[1,20,896]{2,1,0:T(8,128)} async-done(((f32[8,20,896]{2,1,0:T(8,128)}), f32[1,20,896]{2,1,0:T(8,128)}) %reduce-scatter.7.cloned.1.call-update) | async-done | bytes 71696
  261.2 1.6 copy.22
  262.8 36.8 %reduce-scatter.5.cloned.1.call-done = f32[80,896]{1,0:T(8,128)} async-done(((f32[640,896]{1,0:T(8,128)}), f32[80,896]{1,0:T(8,128)}) %reduce-scatter.5.cloned.1.call-update) | async-done | bytes 286736 | tf_op jit(solution)/shard_map/reduce_scatter | solution.py:55
  (22 shorter events, 0.1 us)
Async XLA Ops:
  7.2 205.3 %copy-start = (bf16[384,1280]{1,0:T(8,128)(2,1)S(1)}, bf16[384,1280]{1,0:T(8,128)(2,1)}, u32[]{:S(2)}) copy-start(bf16[384,1280]{1,0:T(8,128)(2,1)} %param.9) | copy-start | bytes 2949124
  7.2 128.6 %all-gather.16.cloned.1.call-start = ((), (), s32[]{:S(2)}) async-start(), calls=%async_computation.7 | async-start | bytes 1179648 | tf_op jit(solution)/shard_map/all_gather | solution.py:40
  20.7 166.3 %all-gather.12.cloned.1.call-start = ((), (), s32[]{:S(2)}) async-start(), calls=%async_computation.4 | async-start | bytes 12386304 | tf_op jit(solution)/shard_map/all_gather | solution.py:21
  23.7 18.6 %copy-start.2 = (bf16[1,128,5120]{2,1,0:T(8,128)(2,1)S(1)}, bf16[1,128,5120]{2,1,0:T(8,128)(2,1)}, u32[]{:S(2)}) copy-start(bf16[1,128,5120]{2,1,0:T(8,128)(2,1)} %param.11) | copy-start | bytes 3932164
  43.2 12.3 %collective-permute-start = (bf16[64,5120]{1,0:T(8,128)(2,1)}, bf16[64,5120]{1,0:T(8,128)(2,1)S(1)}, u32[]{:S(2)}, u32[]{:S(2)}) collective-permute-start(bf16[64,5120]{1,0:T(8,128)(2,1)} %get-tuple-element.11), channel_id=1, source_target_pairs={{0,8},{8,0},{16,24},{24,16},{1,9},{9,1},{17,25},{25,17},{2,10},{10... | collective-permute-start | bytes 1966088 | tf_op jit(solution)/shard_map/ppermute | solution.py:26
  55.5 0.9 copy-start.4
  58.5 10.3 %copy-start.5 = (s32[1,128]{1,0:T(1,128)S(1)}, s32[1,128]{1,0:T(1,128)}, u32[]{:S(2)}) copy-start(s32[1,128]{1,0:T(1,128)} %param.13) | copy-start | bytes 1540
  58.5 10.8 %copy-start.6 = (s32[1,128]{1,0:T(1,128)S(1)}, s32[1,128]{1,0:T(1,128)}, u32[]{:S(2)}) copy-start(s32[1,128]{1,0:T(1,128)} %param.14) | copy-start | bytes 1540
  59.6 44.0 %all-to-all-start = ((bf16[8,64,640]{2,1,0:T(8,128)(2,1)}), bf16[8,64,640]{2,1,0:T(8,128)(2,1)S(1)}, u32[]{:S(2)}, u32[]{:S(2)}) async-start(bf16[8,64,640]{2,1,0:T(8,128)(2,1)} %fusion.58), calls=%async_computation | async-start | bytes 1310720 | tf_op jit(solution)/shard_map/all_to_all | solution.py:33
  68.8 175.2 %all-gather.14.cloned.1.call-start = ((), (), s32[]{:S(2)}) async-start(), calls=%async_computation.6 | async-start | bytes 3276800 | tf_op jit(solution)/shard_map/all_gather | solution.py:36
  68.9 36.4 %collective-permute-start.1 = (s32[64]{0:T(128)S(1)}, s32[64]{0:T(128)S(1)}, u32[]{:S(2)}, u32[]{:S(2)}) collective-permute-start(s32[64]{0:T(128)S(1)} %get-tuple-element.15), channel_id=1, source_target_pairs={{0,8},{8,0},{16,24},{24,16},{1,9},{9,1},{17,25},{25,17},{2,10},{10... | collective-permute-start | bytes 776 | tf_op jit(solution)/shard_map/ppermute | solution.py:26
  103.6 0.9 copy-start.1
  104.4 156.7 %reduce-scatter.7.cloned.1.call-start = ((), (), s32[]{:S(2)}) async-start(), calls=%async_computation.8 | async-start | bytes 774144
  187.0 25.5 %copy-start.3 = (bf16[32,128,128]{2,1,0:T(8,128)(2,1)S(1)}, bf16[32,128,128]{2,1,0:T(8,128)(2,1)}, u32[]{:S(2)}) copy-start(bf16[32,128,128]{2,1,0:T(8,128)(2,1)} %all-gather.16.cloned.1.call-done) | copy-start | bytes 3145732
  227.6 72.0 %reduce-scatter.5.cloned.1.call-start = ((), (), s32[]{:S(2)}) async-start(), calls=%async_computation.5 | async-start | bytes 2580480 | tf_op jit(solution)/shard_map/reduce_scatter | solution.py:55
Sparse Core Ops, SparseCore 0:
  20.8 40.8 all-gather.15
  63.5 123.5 all-gather.11
  188.8 34.0 all-gather.13
  227.7 33.3 reduce-scatter.6
  264.1 35.4 reduce-scatter.4

commit v2 on v1

v2 whole, which is shorter than its diff:
```python
import jax
import jax.numpy as jnp
from jax import lax
from jax.experimental import pallas as pl
from jax.experimental.pallas import tpu as pltpu
from jax.sharding import Mesh, PartitionSpec as P

Z, X, Y, C = 8, 4, 4, 2
MELS, ENC, HID, OUT = 128, 1280, 5120, 3584
FRAMES, SLOTS, SPOTS = 128, 128, 192
BLOCK = OUT // X
WIDE = 512
RROWS = HID // X
ROWS = HID // Z // (Y * C)
AROWS = ENC // Z // (Y * C)
APAD = 24
PART = 2 * ROWS + 2 * APAD
LIVE = 256

bf16, f32, i32 = jnp.bfloat16, jnp.float32, jnp.int32
MESH = pl.DeviceIdType.MESH


def dot(a, b, dims=((1,), (0,))):
    return lax.dot_general(a, b, (dims, ((), ())), preferred_element_type=f32)


def iota(shape, dim):
    return lax.broadcasted_iota(i32, shape, dim)


def one_hot(mask):
    return jnp.where(mask, 1.0, 0.0).astype(bf16)


def kernel(
    mel, convw, bias, hidden, count, vplaces, aplaces, cot,
    out_m, out_a,
    ints, ints_x, ints_all, mel_all, b_all, a_raw, a_all, a_t, windows, conv_t, w_ext,
    spot, picked, merger, audio, aud_send, aud_recv, aud_part, own, core_send, core_recv,
    y_send, y_recv, fin_send, fin_recv, ssem, rsem,
):
    z, x = lax.axis_index("z"), lax.axis_index("x")
    y, core = lax.axis_index("y"), lax.axis_index("core")

    def zmod(v):
        return lax.rem(v + 2 * Z, Z)

    def xmod(v):
        return lax.rem(v + 2 * X, X)

    def ymod(v):
        return lax.rem(v + Y, Y)

    home_x = lax.div(z, 2)
    half = lax.rem(z, 2)

    barrier = pltpu.get_barrier_semaphore()
    peers = [{"z": zmod(z + k)} for k in range(1, Z)]
    peers += [{"x": xmod(x + k)} for k in range(1, X)]
    peers += [{"y": ymod(y + k)} for k in range(1, Y)]
    peers += [{"core": 1 - core}]
    for peer in peers:
        pl.semaphore_signal(barrier, inc=1, device_id=peer, device_id_type=MESH)
    for zl in range(2):
        to_z = 2 * x + zl

        @pl.when(jnp.logical_or(to_z != z, home_x != x))
        def _():
            pl.semaphore_signal(
                barrier, inc=1, device_id={"z": to_z, "x": home_x}, device_id_type=MESH
            )

    pl.semaphore_wait(barrier, len(peers) + 1 + jnp.where(home_x != x, 1, 0))

    sent = []
    names = {}

    def sem(*key):
        return names.setdefault(key, len(names))

    def copy(src, dst, key, device):
        i = sem(*key)
        return pltpu.make_async_remote_copy(
            src_ref=src, dst_ref=dst, send_sem=ssem.at[i], recv_sem=rsem.at[i],
            device_id=device, device_id_type=MESH,
        )

    def send(src, dst, key, device):
        c = copy(src, dst, key, device)
        c.start()
        sent.append(c)

    def arrived(dst, *key):
        copy(dst, dst, key, {"core": 1 - core}).wait_recv()

    def window(zt):
        return pl.ds(pl.multiple_of(lax.div(zt, 2) * BLOCK + lax.rem(zt, 2) * (BLOCK - WIDE), 128), WIDE)

    def b_rows(xs, zs):
        return b_all.at[xs, pl.ds(pl.multiple_of(zs * SPOTS, 64), SPOTS)]

    def a_cols(xt):
        return pl.ds(pl.multiple_of(xt * RROWS, 128), RROWS)

    ints[0:1, :] = aplaces[...]
    ints[1:2, :] = vplaces[...]
    ints[2:3, :] = jnp.broadcast_to(count[...], (1, 128))
    ints[3:8, :] = jnp.zeros((5, 128), i32)
    ints_x[x] = ints[...]
    ints_all[x, z] = ints[...]
    mel_all[x, z] = mel[...]

    for k in range(1, X):
        xt = xmod(x + k)
        send(ints, ints_x.at[x], ("ix", k), {"x": xt})
        send(hidden.at[:, a_cols(xt)], a_raw.at[x], ("a", k), {"x": xt})
    own_a = pltpu.make_async_copy(hidden.at[:, a_cols(x)], a_raw.at[x], ssem.at[sem("own_a")])
    own_a.start()
    own_b = pltpu.make_async_copy(cot.at[:, window(z)], b_rows(x, z), ssem.at[sem("own_b")])
    own_b.start()
    for k in range(1, Z):
        zt = zmod(z + k)
        send(ints, ints_all.at[x, z], ("iz", k), {"z": zt})
        send(mel, mel_all.at[x, z], ("mz", k), {"z": zt})
    for k in (1, 7, 2, 6, 3, 5, 4):
        zt = zmod(z + k)
        send(cot.at[:, window(zt)], b_rows(x, z), ("b", k), {"z": zt})

    right, left = {"x": xmod(x + 1)}, {"x": xmod(x - 1)}

    def b_out(k):
        block = b_rows(x, zmod(z - k))
        send(block, block, ("br", k), right)
        send(block, block, ("bl", k), left)

    own_b.wait()
    b_out(0)

    own_a.wait()
    for k in range(1, X):
        arrived(ints_x.at[xmod(x - k)], "ix", k)
        arrived(a_raw.at[xmod(x - k)], "a", k)

    def selection(held):
        row, col = iota((128, 256), 0), iota((128, 256), 1)
        return one_hot(jnp.where(row < held, row, row - held + 128) == col)

    for j in range(2):
        held = jnp.broadcast_to(ints_x[2 * j, 2:3, :][:, 0:1], (128, 256))
        pair = jnp.concatenate([a_raw[2 * j], a_raw[2 * j + 1]], axis=0)
        a_all[z, j * 128 : (j + 1) * 128, :] = dot(selection(held), pair).astype(bf16)

    up, down = {"z": zmod(z + 1)}, {"z": zmod(z - 1)}
    up_items = [(0, 0), (0, 1), (1, 0), (1, 1), (2, 0), (2, 1), (3, 0)]
    down_items = [(0, 0), (0, 1), (1, 0), (1, 1), (2, 0), (2, 1), (3, 1)]

    def a_rows(zs, j):
        return a_all.at[zs, pl.ds(j * 128, 128)]

    def ring(n):
        for items, name, step, device in ((up_items, "up", -1, up), (down_items, "down", 1, down)):
            t, j = items[n]
            rows = a_rows(zmod(z + step * t), j)
            if t:
                arrived(rows, name, t - 1, j)
            send(rows, rows, (name, t, j), device)

    ring(0)
    ring(1)

    for k in range(1, Z):
        arrived(ints_all.at[x, zmod(z - k)], "iz", k)
        arrived(mel_all.at[x, zmod(z - k)], "mz", k)
    for k in range(1, X):
        xt = xmod(x + k)
        send(ints_all.at[x], ints_all.at[x], ("ixa", k), {"x": xt})
        send(mel_all.at[x], mel_all.at[x], ("mxa", k), {"x": xt})

    b0 = bias[...]
    hi = b0.astype(bf16).astype(f32)
    mid = (b0 - hi).astype(bf16).astype(f32)
    low = b0 - hi - mid
    row = iota((128, ENC), 0)
    w_ext[...] = jnp.where(row == 0, hi, jnp.where(row == 1, mid, jnp.where(row == 2, low, 0.0))).astype(bf16)
    conv_t[:, 0 : 3 * MELS] = convw[...].T
    conv_t[:, 3 * MELS :] = w_ext[...].T

    for k in (1, 7, 2, 6, 3, 5, 4):
        arrived(b_rows(x, zmod(z - k)), "b", k)
        b_out(k)

    for k in range(1, X):
        xs = xmod(x - k)
        arrived(ints_all.at[xs], "ixa", k)
        arrived(mel_all.at[xs], "mxa", k)

    windows[:, 3 * MELS :] = jnp.ones((X * Z * FRAMES, 128), bf16)
    edge = iota((FRAMES, MELS), 0)

    @pl.loop(0, Z)
    def _(zs):
        for xs in range(X):
            own_frames = mel_all[xs, zs].astype(f32)
            zp = zs if xs else jnp.maximum(zs - 1, 0)
            zn = zs if xs < X - 1 else jnp.minimum(zs + 1, Z - 1)
            before = mel_all[(xs - 1) % X, zp].astype(f32)
            after = mel_all[(xs + 1) % X, zn].astype(f32)
            if xs == 0:
                before = jnp.where(jnp.broadcast_to(zs, before.shape) == 0, 0.0, before)
            if xs == X - 1:
                after = jnp.where(jnp.broadcast_to(zs, after.shape) == Z - 1, 0.0, after)
            before = jnp.where(edge == 0, pltpu.roll(before, 1, 0), pltpu.roll(own_frames, 1, 0))
            after = jnp.where(
                edge == FRAMES - 1, pltpu.roll(after, FRAMES - 1, 0), pltpu.roll(own_frames, FRAMES - 1, 0)
            )
            at = pl.ds(pl.multiple_of((xs * Z + zs) * FRAMES, FRAMES), FRAMES)
            windows[at, 0:MELS] = before.astype(bf16)
            windows[at, MELS : 2 * MELS] = own_frames.astype(bf16)
            windows[at, 2 * MELS : 3 * MELS] = after.astype(bf16)

    @pl.loop(0, Z)
    def _(zs):
        for j in range(2):
            held = jnp.broadcast_to(ints_all[2 * j, zs, 2:3, :][:, 0:1], (128, 256))
            pick = selection(held)
            places = jnp.concatenate([ints_all[2 * j, zs, 1:2, :], ints_all[2 * j + 1, zs, 1:2, :]], axis=1)
            high = lax.shift_right_logical(places, 7)
            rest = jnp.bitwise_and(places, 127)
            high = jnp.broadcast_to(high.astype(f32), (128, 256)).astype(bf16)
            rest = jnp.broadcast_to(rest.astype(f32), (128, 256)).astype(bf16)
            value = 128.0 * dot(pick, high, ((1,), (1,))) + dot(pick, rest, ((1,), (1,)))
            spot[pl.ds(pl.multiple_of(zs * LIVE + j * 128, 128), 128), :] = value.astype(i32)

    ring(2)

    audio[...] = jnp.zeros_like(audio)

    def audio_piece(h):
        wpos = []
        for zs in (2 * h, 2 * h + 1):
            base = (zs * X + x) * SPOTS
            here = iota((SPOTS, 128), 0) + base
            total = jnp.zeros((SPOTS, 4 * MELS), f32)

            def shard(xs, total):
                hot = jnp.concatenate(
                    [
                        one_hot(jnp.broadcast_to(ints_all[xs, zt, 0:1, :], (SPOTS, 128)) == here)
                        for zt in range(Z)
                    ],
                    axis=1,
                )
                at = pl.ds(pl.multiple_of(xs * (Z * FRAMES), FRAMES), Z * FRAMES)
                return total + dot(hot, windows[at, :])

            wpos.append(lax.fori_loop(0, X, shard, total).astype(bf16))
        wpos = jnp.concatenate(wpos, axis=0)
        bs = b_all[x, h * 2 * SPOTS : (h + 1) * 2 * SPOTS, :]

        @pl.loop(0, ENC // 256)
        def _(m):
            at = pl.ds(pl.multiple_of(m * 256, 256), 256)
            conv = dot(conv_t[at, :], wpos, ((1,), (1,)))
            act = (0.5 * conv * (1.0 + lax.erf(conv * 0.7071067811865476))).astype(bf16)
            audio[at, :] += dot(act, bs)

    def forward(ks):
        for k in ks:
            zs = zmod(z - k)
            block = b_rows(xmod(x - 1), zs)
            arrived(block, "br", k)
            if k < 4:
                send(block, block, ("fr", k), right)
            block = b_rows(xmod(x + 1), zs)
            arrived(block, "bl", k)
            if k >= 4:
                send(block, block, ("fl", k), left)

    audio_piece(0)
    ring(3)
    forward((0, 1, 7))
    audio_piece(1)
    ring(4)
    forward((2, 6))
    audio_piece(2)
    ring(5)
    forward((3, 5, 4))
    audio_piece(3)
    ring(6)

    for k in range(1, X):
        xt = xmod(x + k)
        aud_send[k] = audio[pl.ds(pl.multiple_of(xt * (ENC // X), 64), ENC // X), :].astype(bf16)
        send(aud_send.at[k], aud_recv.at[k], ("aud", k), {"x": xt})

    lane = iota((256, 128), 1)

    def pick_rows(xs, part, first):
        span = 4 * SPOTS

        @pl.loop(0, Z)
        def _(q):
            at = pl.ds(pl.multiple_of(q * LIVE, LIVE), LIVE)
            spots = spot[at, :]
            tiles = []
            for t in range(span // 128):
                ends = []
                for s in (2 * t, 2 * t + 1):
                    ends.append((4 * part + s // 3) * X * SPOTS + (s % 3) * 64)
                there = jnp.where(lane < 64, lane + ends[0], lane - 64 + ends[1]) + xs * SPOTS
                tiles.append(one_hot(spots == there))
            got = dot(jnp.concatenate(tiles, axis=1), b_all[xs, part * span : (part + 1) * span, :])
            if first:
                picked[at, :] = got
            else:
                picked[at, :] += got

    pick_rows(x, 0, True)
    pick_rows(x, 1, False)
    pick_rows(xmod(x - 1), 0, False)
    pick_rows(xmod(x - 1), 1, False)
    pick_rows(xmod(x + 1), 0, False)
    pick_rows(xmod(x + 1), 1, False)

    for t in range(3):
        for j in range(2):
            if (t + 1, j) not in up_items:
                arrived(a_rows(zmod(z - t - 1), j), "up", t, j)
            if (t + 1, j) not in down_items:
                arrived(a_rows(zmod(z + t + 1), j), "down", t, j)
    arrived(a_rows(zmod(z + 4), 0), "up", 3, 0)
    arrived(a_rows(zmod(z + 4), 1), "down", 3, 1)

    @pl.loop(0, Z)
    def _(zs):
        for j in range(2):
            a_t[:, pl.ds(pl.multiple_of(zs * LIVE + j * 128, 128), 128)] = a_all[
                zs, j * 128 : (j + 1) * 128, :
            ].T

    for k in range(Z):
        arrived(b_rows(xmod(x + 2), zmod(z - k)), "fr" if k < 4 else "fl", k)
    pick_rows(xmod(x + 2), 0, False)
    pick_rows(xmod(x + 2), 1, False)

    total = audio[pl.ds(pl.multiple_of(x * (ENC // X), 64), ENC // X), :]
    for k in range(1, X):
        arrived(aud_recv.at[k], "aud", k)
        total = total + aud_recv[k].astype(f32)
    audio[0 : ENC // X, :] = total
    aud_part[...] = jnp.zeros_like(aud_part)
    for zl in range(2):
        for d in range(Y * C):
            at = (zl * Y * C + d) * AROWS
            aud_part[d, zl * APAD : zl * APAD + AROWS, :] = audio[at : at + AROWS, :]

    @pl.loop(0, RROWS // 256)
    def _(m):
        at = pl.ds(pl.multiple_of(m * 256, 256), 256)
        merger[at, :] = dot(a_t[at, :], picked[...].astype(bf16))

    def merger_rows(zl, d):
        return merger[pl.ds(pl.multiple_of((zl * Y * C + d) * ROWS, 16), ROWS), :]

    other = 1 - core
    for yt in range(Y):
        for zl in range(2):
            core_send[yt, zl * ROWS : (zl + 1) * ROWS, :] = merger_rows(zl, 2 * yt + other).astype(bf16)
            own[yt, zl * ROWS : (zl + 1) * ROWS, :] = merger_rows(zl, 2 * yt + core)
        core_send[yt, 2 * ROWS :, :] = aud_part[2 * yt + other].astype(bf16)
        own[yt, 2 * ROWS :, :] = aud_part[2 * yt + core]
    send(core_send, core_recv, ("core",), {"core": other})
    arrived(core_recv, "core")
    for k in range(1, Y):
        yt = ymod(y + k)
        y_send[k] = (own[yt] + core_recv[yt].astype(f32)).astype(bf16)
        send(y_send.at[k], y_recv.at[k], ("y", k), {"y": yt})
    total = own[y] + core_recv[y].astype(f32)
    for k in range(1, Y):
        arrived(y_recv.at[k], "y", k)
        total = total + y_recv[k].astype(f32)
    for zl in range(2):
        fin_send[zl, 0:ROWS, :] = total[zl * ROWS : (zl + 1) * ROWS]
        fin_send[zl, ROWS:, :] = total[2 * ROWS + zl * APAD : 2 * ROWS + (zl + 1) * APAD]

    fin = sem("fin", 0), sem("fin", 1)
    fin_out = sem("fout", 0), sem("fout", 1)
    for zl in range(2):
        to_z = 2 * x + zl
        elsewhere = jnp.logical_or(to_z != z, home_x != x)
        out = pltpu.make_async_remote_copy(
            src_ref=fin_send.at[zl], dst_ref=fin_recv.at[half], send_sem=ssem.at[fin_out[zl]],
            recv_sem=rsem.at[fin[0] + half], device_id={"z": to_z, "x": home_x}, device_id_type=MESH,
        )

        @pl.when(elsewhere)
        def _():
            out.start()

        @pl.when(jnp.logical_not(elsewhere))
        def _():
            fin_recv[half] = fin_send[zl]

    for h in range(2):
        @pl.when(jnp.logical_or(2 * x + h != z, home_x != x))
        def _():
            arrived(fin_recv.at[h], "fin", h)

    out_m[:, 0:WIDE] = fin_recv[0, 0:ROWS, :]
    out_m[:, WIDE:] = fin_recv[1, 0:ROWS, 2 * WIDE - BLOCK :]
    out_a[:, 0:WIDE] = fin_recv[0, ROWS : ROWS + AROWS, :]
    out_a[:, WIDE:] = fin_recv[1, ROWS : ROWS + AROWS, 2 * WIDE - BLOCK :]

    for c in sent:
        c.wait_send()
    for zl in range(2):
        to_z = 2 * x + zl

        @pl.when(jnp.logical_or(to_z != z, home_x != x))
        def _():
            pltpu.make_async_remote_copy(
                src_ref=fin_send.at[zl], dst_ref=fin_recv.at[half], send_sem=ssem.at[fin_out[zl]],
                recv_sem=rsem.at[fin[0] + half], device_id={"z": to_z, "x": home_x}, device_id_type=MESH,
            ).wait_send()

    assert len(names) <= 128


def local(mel, conv_weight, conv_bias, video_hidden, video_count, video_places, audio_places, cotangent):
    vmem = pl.BlockSpec(memory_space=pltpu.VMEM)
    hbm = pl.BlockSpec(memory_space=pl.ANY)
    part = (PART, WIDE)
    merger, audio = pl.pallas_call(
        kernel,
        out_shape=(
            jax.ShapeDtypeStruct((ROWS, BLOCK), f32),
            jax.ShapeDtypeStruct((AROWS, BLOCK), f32),
        ),
        in_specs=[vmem, vmem, vmem, hbm, vmem, vmem, vmem, hbm],
        out_specs=(vmem, vmem),
        scratch_shapes=[
            pltpu.VMEM((8, 128), i32),
            pltpu.VMEM((X, 8, 128), i32),
            pltpu.VMEM((X, Z, 8, 128), i32),
            pltpu.VMEM((X, Z, FRAMES, MELS), bf16),
            pltpu.VMEM((X, Z * SPOTS, WIDE), bf16),
            pltpu.VMEM((X, SLOTS, RROWS), bf16),
            pltpu.VMEM((Z, LIVE, RROWS), bf16),
            pltpu.VMEM((RROWS, Z * LIVE), bf16),
            pltpu.VMEM((X * Z * FRAMES, 4 * MELS), bf16),
            pltpu.VMEM((ENC, 4 * MELS), bf16),
            pltpu.VMEM((128, ENC), bf16),
            pltpu.VMEM((Z * LIVE, 128), i32),
            pltpu.VMEM((Z * LIVE, WIDE), f32),
            pltpu.VMEM((RROWS, WIDE), f32),
            pltpu.VMEM((ENC, WIDE), f32),
            pltpu.VMEM((X, ENC // X, WIDE), bf16),
            pltpu.VMEM((X, ENC // X, WIDE), bf16),
            pltpu.VMEM((Y * C, 2 * APAD, WIDE), f32),
            pltpu.VMEM((Y, *part), f32),
            pltpu.VMEM((Y, *part), bf16),
            pltpu.VMEM((Y, *part), bf16),
            pltpu.VMEM((Y, *part), bf16),
            pltpu.VMEM((Y, *part), bf16),
            pltpu.VMEM((2, ROWS + APAD, WIDE), f32),
            pltpu.VMEM((2, ROWS + APAD, WIDE), f32),
            pltpu.SemaphoreType.DMA((128,)),
            pltpu.SemaphoreType.DMA((128,)),
        ],
        compiler_params=pltpu.CompilerParams(
            collective_id=0, has_side_effects=True, vmem_limit_bytes=60 * 2**20
        ),
    )(
        mel[0], conv_weight, conv_bias[None], video_hidden[0],
        video_count, video_places, audio_places, cotangent[0],
    )
    return merger[None], audio[None]


def solution(mesh):
    whole = Mesh(mesh.devices.reshape(Z, X, Y, C), ("z", "x", "y", "core"))
    dp, ctx = ("y", "core"), ("z", "x")
    return jax.shard_map(
        local,
        mesh=whole,
        in_specs=(
            P(dp, ctx, None),
            P(),
            P(),
            P(dp, ctx, None),
            P(dp, ctx),
            P(dp, ctx),
            P(dp, ctx),
            P(dp, ctx, None),
        ),
        out_specs=(P(ctx, dp, None), P(ctx, dp, None)),
        check_vma=False,
    )
```

time: 307 us -> 176 us (0.57)
  Pallas kernels: 0 us -> 168 us
  waiting for transfers between devices: 105 us -> 0 us
  blocking collectives: 95.6 us -> 0 us
  local copies, waits for them, and re-layouts: 56.5 us -> 4.58 us
  matrix products: 20.4 us -> 0 us
  between operations: 14.6 us -> 1.29 us
  starting transfers between devices: 11.3 us -> 0 us
    pallas_call x0 -> x1, Pallas kernels: none -> 168 us  [local(): pl.pallas_call(kernel, out_shape=(jax.ShapeDtypeStruct((ROWS, BLOCK), f32...]
    all_gather x5 -> x0, blocking collectives: 77.1 us -> none  [the longest x2 29.5 us: local(): spots = lax.all_gather(lax.all_gather(spots, 'x'), 'z').reshape(-1)]
    all_gather x3 -> x0, waiting for transfers between devices: 48.1 us -> none  [the longest x1 48.1 us: local(): up = lax.all_gather(cols, 'z', tiled=True).reshape(-1, block_cols)]
    gather x4 -> x0, local copies, waits for them, and re-layouts: 43.2 us -> none  [the longest x1 25.4 us: local(): jnp.take(up, audio_spots, axis=0)]
    reduce_scatter x1 -> x0, waiting for transfers between devices: 36.8 us -> none  [local(): merger = lax.psum_scatter(merger, ('y', 'core'), tiled=True)]
    dot_general x2 -> x0, matrix products: 20.4 us -> none  [the longest x1 13.2 us: local(): lax.dot_general(audio, jnp.take(up, audio_spots, axis=0), contract, prefe...]
    all_to_all x1 -> x0, blocking collectives: 18.5 us -> none  [local(): lax.all_to_all(jnp.transpose(upstream.reshape(-1, GRID_COLS, block_cols),...]
    ppermute x2 -> x0, waiting for transfers between devices: 10.4 us -> none  [local(): lax.ppermute((hidden[middle:], places[middle:]), 'x', pairs)]
  transfers between devices with their start and end apart: 8 -> 0, of which waited for: 4 -> 0; matrix products, arithmetic and copies ran while one was open for 25% -> 0% of each run, Pallas kernels for 0% -> 0%
where the time goes in v2:
time: 176 us; the launch traced here: 174 us
  Pallas kernels  168 us (95%)
  local copies, waits for them, and re-layouts  4.58 us (3%)
    pallas_call x1, Pallas kernels, local(): pl.pallas_call(kernel, out_shape=(jax.ShapeDtypeStruct((ROWS, BLOCK), f32...  168 us

profile of v2, /device:TPU:6, one launch (start us, length us, event | category | flops | bytes accessed | tf_op | source)
XLA Modules:
  0.0 173.6 jit_solution(11168207707330890569)
XLA Ops:
  1.3 1.3 broadcast_in_dim.9.bias
  2.6 167.8 %shard_map.95 = (f32[80,896]{1,0:T(8,128)}, f32[20,896]{1,0:T(8,128)}) custom-call(bf16[128,128]{1,0:T(8,128)(2,1)} %bitcast.9, bf16[384,1280]{1,0:T(8,128)(2,1)} %convw.1, f32[1,1280]{1,0:T(1,128)} %broadcast_in_dim.9.bias, bf16[128,5120]{1,0:T(8,128)(2,1)} %bitcast.6, s32[1,1]{1,0:T(1,128)S(6)} %copy.12.count, s32[1,128]{1,0:T(1,128)} %vplaces.1, ...), custom_call_target="tpu_custom_call" | custom-call | tf_op jit(solution)/shard_map/pallas_call | solution.py:434
  170.4 1.6 copy.10
  172.0 1.7 copy.13

commit v3 on v2

v3 whole, which is shorter than its diff:
```python
import jax
import jax.numpy as jnp
from jax import lax
from jax.experimental import pallas as pl
from jax.experimental.pallas import tpu as pltpu
from jax.sharding import Mesh, PartitionSpec as P

Z, X, Y, C = 8, 4, 4, 2
MELS, ENC, HID, OUT = 128, 1280, 5120, 3584
FRAMES, SLOTS, SPOTS = 128, 128, 192
BLOCK = OUT // X
WIDE = 512
RROWS = HID // X
ROWS = HID // Z // (Y * C)
AROWS = ENC // Z // (Y * C)
APAD = 32
PART = ROWS + APAD
KEEP = 24
HALF = 256
EROWS = ENC // Z
ZROWS = HID // Z
LIVE = 256

bf16, f32, i32 = jnp.bfloat16, jnp.float32, jnp.int32
MESH = pl.DeviceIdType.MESH


def dot(a, b, dims=((1,), (0,))):
    return lax.dot_general(a, b, (dims, ((), ())), preferred_element_type=f32)


def iota(shape, dim):
    return lax.broadcasted_iota(i32, shape, dim)


def one_hot(mask):
    return jnp.where(mask, 1.0, 0.0).astype(bf16)


def kernel(
    mel, convw, bias, hidden, count, vplaces, aplaces, cot,
    out_m, out_a,
    ints, ints_x, ints_all, mel_all, b_all, a_raw, a_all, a_t, windows, conv_t, w_ext,
    spot, picked, picked_b, merger, acts, audio, aud_send, aud_relay, aud_recv, aud_part, own, core_send, core_recv,
    y_send, y_relay, y_recv, fin_send, fin_recv, fina_send, fina_recv, a_relay, b_relay, ssem, rsem,
):
    z, x = lax.axis_index("z"), lax.axis_index("x")
    y, core = lax.axis_index("y"), lax.axis_index("core")

    def zmod(v):
        return lax.rem(v + 2 * Z, Z)

    def xmod(v):
        return lax.rem(v + 2 * X, X)

    def ymod(v):
        return lax.rem(v + Y, Y)

    home_x = lax.div(z, 2)
    half = lax.rem(z, 2)

    barrier = pltpu.get_barrier_semaphore()
    peers = [{"z": zmod(z + k)} for k in range(1, Z)]
    peers += [{"x": xmod(x + k)} for k in range(1, X)]
    peers += [{"y": ymod(y + k)} for k in range(1, Y)]
    peers += [{"core": 1 - core}]
    for peer in peers:
        pl.semaphore_signal(barrier, inc=1, device_id=peer, device_id_type=MESH)
    for h in range(2):

        @pl.when(jnp.logical_or(2 * x + h != z, lax.rem(z, X) != x))
        def _():
            pl.semaphore_signal(
                barrier, inc=1, device_id={"z": 2 * x + h, "x": lax.rem(z, X)}, device_id_type=MESH
            )

    here = jnp.logical_and(home_x == x, lax.rem(z, X) == x)
    pl.semaphore_wait(barrier, len(peers) + 2 - jnp.where(here, 1, 0))

    sent = []
    names = {}

    def sem(*key):
        return names.setdefault(key, len(names))

    def copy(src, dst, key, device):
        i = sem(*key)
        return pltpu.make_async_remote_copy(
            src_ref=src, dst_ref=dst, send_sem=ssem.at[i], recv_sem=rsem.at[i],
            device_id=device, device_id_type=MESH,
        )

    def send(src, dst, key, device):
        c = copy(src, dst, key, device)
        c.start()
        sent.append(c)

    def arrived(dst, *key):
        copy(dst, dst, key, {"core": 1 - core}).wait_recv()

    def window(zt):
        return pl.ds(pl.multiple_of(lax.div(zt, 2) * BLOCK + lax.rem(zt, 2) * (BLOCK - WIDE), 128), WIDE)

    def b_rows(xs, zs):
        return b_all.at[xs, pl.ds(pl.multiple_of(zs * SPOTS, 64), SPOTS)]

    def b_half(zs, h):
        return b_all.at[x, pl.ds(pl.multiple_of(zs * SPOTS + h * 96, 32), 96)]

    def a_cols(xt, w):
        return hidden.at[:, pl.ds(pl.multiple_of((xt + X * w) * ZROWS, 128), ZROWS)]

    def a_slot(xs, w):
        return a_raw.at[xs, :, pl.ds(w * ZROWS, ZROWS)]

    right, left = {"x": xmod(x + 1)}, {"x": xmod(x - 1)}
    sides = ((1, right), (-1, left))

    ints[0:1, :] = aplaces[...]
    ints[1:2, :] = vplaces[...]
    ints[2:3, :] = jnp.broadcast_to(count[...], (1, 128))
    ints[3:8, :] = jnp.zeros((5, 128), i32)
    ints_x[x] = ints[...]
    ints_all[x, z] = ints[...]
    mel_all[x, z] = mel[...]

    for k in range(1, Z):
        zt = zmod(z + k)
        send(ints, ints_all.at[x, z], ("iz", k), {"z": zt})
        send(mel, mel_all.at[x, z], ("mz", k), {"z": zt})
    for k in range(1, X):
        send(ints, ints_x.at[x], ("ix", k), {"x": xmod(x + k)})
    for w, (step, side) in enumerate(sides):
        send(a_cols(xmod(x + 2), w), a_relay.at[w], ("a2", w), side)
    for step, side in sides:
        for w in range(2):
            send(a_cols(xmod(x + step), w), a_slot(x, w), ("a", step, w), side)
    own_a = []
    for w in range(2):
        c = pltpu.make_async_copy(a_cols(x, w), a_slot(x, w), ssem.at[sem("own_a", w)])
        c.start()
        own_a.append(c)
    own_b = pltpu.make_async_copy(cot.at[:, window(z)], b_rows(x, z), ssem.at[sem("own_b")])
    own_b.start()
    zt = zmod(z + 4)
    send(cot.at[pl.ds(96, 96), window(zt)], b_relay, ("b4",), {"z": zmod(z - 1)})
    for k in (1, 7, 2, 6, 3, 5):
        zt = zmod(z + k)
        send(cot.at[:, window(zt)], b_rows(x, z), ("b", k), {"z": zt})
    zt = zmod(z + 4)
    send(cot.at[pl.ds(0, 96), window(zt)], b_half(z, 0), ("b", 4), {"z": zt})

    def b_out(k):
        block = b_rows(x, zmod(z - k))
        send(block, block, ("br", k), right)
        send(block, block, ("bl", k), left)


    def selection(held):
        row, col = iota((128, 256), 0), iota((128, 256), 1)
        return one_hot(jnp.where(row < held, row, row - held + 128) == col)

    up, down = {"z": zmod(z + 1)}, {"z": zmod(z - 1)}
    up_items = [(0, 0), (0, 1), (1, 0), (1, 1), (2, 0), (2, 1), (3, 0)]
    down_items = [(0, 0), (0, 1), (1, 0), (1, 1), (2, 0), (2, 1), (3, 1)]

    def pair(j):
        return lax.rem(lax.div(x, 2) + j, 2)

    def a_rows(zs, j):
        return a_all.at[zs, pl.ds(pl.multiple_of(pair(j) * 128, 128), 128)]

    def pack(j):
        p = pair(j)
        held = jnp.broadcast_to(ints_x[2 * p, 2:3, :][:, 0:1], (128, 256))
        both = jnp.concatenate([a_raw[2 * p], a_raw[2 * p + 1]], axis=0)
        a_all[z, pl.ds(pl.multiple_of(p * 128, 128), 128), :] = dot(selection(held), both).astype(bf16)

    def ring(n):
        for items, name, step, device in ((up_items, "up", -1, up), (down_items, "down", 1, down)):
            t, j = items[n]
            rows = a_rows(zmod(z + step * t), j)
            if t:
                arrived(rows, name, t - 1, j)
            send(rows, rows, (name, t, j), device)

    for w, (step, side) in enumerate(sides):
        arrived(a_relay.at[w], "a2", w)
        send(a_relay.at[w], a_slot(xmod(x - step), w), ("a3", w), side)
    own_b.wait()
    b_out(0)

    b0 = bias[...]
    hi = b0.astype(bf16).astype(f32)
    mid = (b0 - hi).astype(bf16).astype(f32)
    low = b0 - hi - mid
    row = iota((128, ENC), 0)
    w_ext[...] = jnp.where(row == 0, hi, jnp.where(row == 1, mid, jnp.where(row == 2, low, 0.0))).astype(bf16)
    conv_t[:, 0 : 3 * MELS] = convw[...].T
    conv_t[:, 3 * MELS :] = w_ext[...].T

    for k in range(1, Z):
        arrived(ints_all.at[x, zmod(z - k)], "iz", k)
        arrived(mel_all.at[x, zmod(z - k)], "mz", k)
    def mel_half(xs, w):
        return mel_all.at[xs, pl.ds(w * (Z // 2), Z // 2)]

    for k in range(1, X):
        send(ints_all.at[x], ints_all.at[x], ("ixa", k), {"x": xmod(x + k)})
    for w in range(2):
        for step, side in sides:
            send(mel_half(x, w), mel_half(x, w), ("mxa", step, w), side)

    for c in own_a:
        c.wait()
    for k in range(1, X):
        arrived(ints_x.at[xmod(x - k)], "ix", k)
    for w, (step, side) in enumerate(sides):
        for v in range(2):
            arrived(a_slot(xmod(x - step), v), "a", step, v)
    pack(0)
    ring(0)
    for w in range(2):
        arrived(a_slot(xmod(x + 2), w), "a3", w)
    pack(1)
    ring(1)

    def forward(ks):
        for k in ks:
            zs = zmod(z - k)
            block = b_rows(xmod(x - 1), zs)
            arrived(block, "br", k)
            if k < 4:
                send(block, block, ("fr", k), right)
            block = b_rows(xmod(x + 1), zs)
            arrived(block, "bl", k)
            if k >= 4:
                send(block, block, ("fl", k), left)

    def audio_piece(h):
        wpos = []
        for zs in (2 * h, 2 * h + 1):
            base = (zs * X + x) * SPOTS
            here = iota((SPOTS, 128), 0) + base
            total = jnp.zeros((SPOTS, 4 * MELS), f32)

            def shard(xs, total):
                hot = jnp.concatenate(
                    [
                        one_hot(jnp.broadcast_to(ints_all[xs, zt, 0:1, :], (SPOTS, 128)) == here)
                        for zt in range(Z)
                    ],
                    axis=1,
                )
                at = pl.ds(pl.multiple_of(xs * (Z * FRAMES), FRAMES), Z * FRAMES)
                return total + dot(hot, windows[at, :])

            wpos.append(lax.fori_loop(0, X, shard, total).astype(bf16))
        wpos = jnp.concatenate(wpos, axis=0)

        @pl.loop(0, ENC // 256)
        def _(m):
            at = pl.ds(pl.multiple_of(m * 256, 256), 256)
            conv = dot(conv_t[at, :], wpos, ((1,), (1,)))
            act = (0.5 * conv * (1.0 + lax.erf(conv * 0.7071067811865476))).astype(bf16)
            acts[at, h * 2 * SPOTS : (h + 1) * 2 * SPOTS] = act

    def b_in(ks):
        for k in ks:
            arrived(b_rows(x, zmod(z - k)), "b", k)
            b_out(k)

    for w, (step, side) in enumerate(sides):
        rows = mel_half(xmod(x - step), w)
        arrived(rows, "mxa", step, w)
        send(rows, rows, ("mxb", w), side)
    arrived(b_relay, "b4")
    send(b_relay, b_half(zmod(z + 1), 1), ("b5",), {"z": zmod(z - 3)})
    for k in (1, 7):
        arrived(b_rows(x, zmod(z - k)), "b", k)
        b_out(k)

    forward((0,))
    for k in range(1, X):
        arrived(ints_all.at[xmod(x - k)], "ixa", k)
    for w, (step, side) in enumerate(sides):
        arrived(mel_half(xmod(x - step), 1 - w), "mxa", step, 1 - w)
        arrived(mel_half(xmod(x + 2), w), "mxb", w)

    windows[:, 3 * MELS :] = jnp.ones((X * Z * FRAMES, 128), bf16)
    edge = iota((FRAMES, MELS), 0)

    @pl.loop(0, Z)
    def _(zs):
        for xs in range(X):
            own_frames = mel_all[xs, zs].astype(f32)
            zp = zs if xs else jnp.maximum(zs - 1, 0)
            zn = zs if xs < X - 1 else jnp.minimum(zs + 1, Z - 1)
            before = mel_all[(xs - 1) % X, zp].astype(f32)
            after = mel_all[(xs + 1) % X, zn].astype(f32)
            if xs == 0:
                before = jnp.where(jnp.broadcast_to(zs, before.shape) == 0, 0.0, before)
            if xs == X - 1:
                after = jnp.where(jnp.broadcast_to(zs, after.shape) == Z - 1, 0.0, after)
            before = jnp.where(edge == 0, pltpu.roll(before, 1, 0), pltpu.roll(own_frames, 1, 0))
            after = jnp.where(
                edge == FRAMES - 1, pltpu.roll(after, FRAMES - 1, 0), pltpu.roll(own_frames, FRAMES - 1, 0)
            )
            at = pl.ds(pl.multiple_of((xs * Z + zs) * FRAMES, FRAMES), FRAMES)
            windows[at, 0:MELS] = before.astype(bf16)
            windows[at, MELS : 2 * MELS] = own_frames.astype(bf16)
            windows[at, 2 * MELS : 3 * MELS] = after.astype(bf16)

    b_in((2, 6))

    @pl.loop(0, Z)
    def _(zs):
        for j in range(2):
            held = jnp.broadcast_to(ints_all[2 * j, zs, 2:3, :][:, 0:1], (128, 256))
            pick = selection(held)
            places = jnp.concatenate([ints_all[2 * j, zs, 1:2, :], ints_all[2 * j + 1, zs, 1:2, :]], axis=1)
            high = lax.shift_right_logical(places, 7)
            rest = jnp.bitwise_and(places, 127)
            high = jnp.broadcast_to(high.astype(f32), (128, 256)).astype(bf16)
            rest = jnp.broadcast_to(rest.astype(f32), (128, 256)).astype(bf16)
            value = 128.0 * dot(pick, high, ((1,), (1,))) + dot(pick, rest, ((1,), (1,)))
            spot[pl.ds(pl.multiple_of(zs * LIVE + j * 128, 128), 128), :] = value.astype(i32)

    ring(2)
    b_in((3, 5))
    forward((1, 7))
    audio_piece(0)
    arrived(b_half(zmod(z - 4), 0), "b", 4)
    arrived(b_half(zmod(z + 4), 1), "b5")
    b_out(4)
    ring(3)
    forward((2, 6))
    audio_piece(1)
    ring(4)
    forward((3, 5))
    audio_piece(2)
    ring(5)
    forward((4,))
    audio_piece(3)

    @pl.loop(0, ENC // 256)
    def _(m):
        at = pl.ds(pl.multiple_of(m * 256, 256), 256)
        audio[at, :] = dot(acts[at, :], b_all[x])

    def audio_rows(xt, w):
        rows = [
            audio[pl.ds(pl.multiple_of((xt + X * zl) * EROWS, 32), EROWS), w * HALF : (w + 1) * HALF]
            for zl in range(2)
        ]
        return jnp.concatenate(rows, axis=0)

    for w, (step, side) in enumerate(sides):
        aud_send[0, w] = audio_rows(xmod(x + 2), w).astype(bf16)
        send(aud_send.at[0, w], aud_relay.at[w], ("aud1", w), side)
        aud_send[1, w] = audio_rows(xmod(x + step), 1 - w).astype(bf16)
        send(aud_send.at[1, w], aud_recv.at[1, w], ("aud2", w), side)

    def audio_relay():
        for w, (step, side) in enumerate(sides):
            arrived(aud_relay.at[w], "aud1", w)
            aud_send[2, w] = (audio_rows(xmod(x + step), w) + aud_relay[w].astype(f32)).astype(bf16)
            send(aud_send.at[2, w], aud_recv.at[0, w], ("aud3", w), side)

    lane = iota((256, 128), 1)

    def pick_rows(xs, part, first):
        span = 4 * SPOTS

        @pl.loop(0, Z)
        def _(q):
            at = pl.ds(pl.multiple_of(q * LIVE, LIVE), LIVE)
            spots = spot[at, :]
            tiles = []
            for t in range(span // 128):
                ends = []
                for s in (2 * t, 2 * t + 1):
                    ends.append((4 * part + s // 3) * X * SPOTS + (s % 3) * 64)
                there = jnp.where(lane < 64, lane + ends[0], lane - 64 + ends[1]) + xs * SPOTS
                tiles.append(one_hot(spots == there))
            got = dot(jnp.concatenate(tiles, axis=1), b_all[xs, part * span : (part + 1) * span, :])
            if first:
                picked[at, :] = got
            else:
                picked[at, :] += got

    ring(6)
    pick_rows(x, 0, True)
    pick_rows(x, 1, False)
    audio_relay()
    pick_rows(xmod(x - 1), 0, False)
    pick_rows(xmod(x - 1), 1, False)
    pick_rows(xmod(x + 1), 0, False)
    pick_rows(xmod(x + 1), 1, False)

    for t in range(3):
        for j in range(2):
            if (t + 1, j) not in up_items:
                arrived(a_rows(zmod(z - t - 1), j), "up", t, j)
            if (t + 1, j) not in down_items:
                arrived(a_rows(zmod(z + t + 1), j), "down", t, j)
    arrived(a_rows(zmod(z + 4), 0), "up", 3, 0)
    arrived(a_rows(zmod(z + 4), 1), "down", 3, 1)

    @pl.loop(0, Z)
    def _(zs):
        for j in range(2):
            a_t[:, pl.ds(pl.multiple_of(zs * LIVE + j * 128, 128), 128)] = a_all[
                zs, j * 128 : (j + 1) * 128, :
            ].T

    for k in range(Z):
        arrived(b_rows(xmod(x + 2), zmod(z - k)), "fr" if k < 4 else "fl", k)
    pick_rows(xmod(x + 2), 0, False)
    pick_rows(xmod(x + 2), 1, False)

    aud_part[...] = jnp.zeros_like(aud_part)
    sums = []
    for w in range(2):
        arrived(aud_recv.at[0, w], "aud3", w)
        arrived(aud_recv.at[1, 1 - w], "aud2", 1 - w)
        sums.append(audio_rows(x, w) + aud_recv[0, w].astype(f32) + aud_recv[1, 1 - w].astype(f32))
    audio[0 : 2 * EROWS, :] = jnp.concatenate(sums, axis=1)
    for zl in range(2):
        for d in range(Y * C):
            at = zl * EROWS + d * AROWS
            aud_part[zl, d, 0:AROWS, :] = audio[at : at + AROWS, :]

    picked_b[...] = picked[...].astype(bf16)
    other = 1 - core

    for zl in range(2):
        for m in range(2):
            at = pl.ds(zl * ZROWS + m * (ZROWS // 2), ZROWS // 2)
            merger[at, :] = dot(a_t[at, :], picked_b[...])

        def merger_rows(d):
            return merger[pl.ds(pl.multiple_of(zl * ZROWS + d * ROWS, 16), ROWS), :]

        for yt in range(Y):
            core_send[zl, yt, 0:ROWS, :] = merger_rows(2 * yt + other)
            core_send[zl, yt, ROWS:, :] = aud_part[zl, 2 * yt + other]
        send(core_send.at[zl], core_recv.at[zl], ("core", zl), {"core": other})
        for yt in range(Y):
            own[zl, yt, 0:ROWS, :] = merger_rows(2 * yt + core)
            own[zl, yt, ROWS:, :] = aud_part[zl, 2 * yt + core]

    y_sides = ((1, {"y": ymod(y + 1)}), (-1, {"y": ymod(y + Y - 1)}))

    def y_part(zl, yt, w):
        cols = slice(w * HALF, (w + 1) * HALF)
        return own[zl, yt, :, cols] + core_recv[zl, yt, :, cols]

    for zl in range(2):
        arrived(core_recv.at[zl], "core", zl)
        for w, (step, side) in enumerate(y_sides):
            y_send[zl, 0, w] = y_part(zl, ymod(y + 2), w).astype(bf16)
            send(y_send.at[zl, 0, w], y_relay.at[zl, w], ("y1", zl, w), side)
        for w, (step, side) in enumerate(y_sides):
            y_send[zl, 1, w] = y_part(zl, ymod(y + Y + step), 1 - w).astype(bf16)
            send(y_send.at[zl, 1, w], y_recv.at[zl, 1, w], ("y2", zl, w), side)
    for zl in range(2):
        for w, (step, side) in enumerate(y_sides):
            arrived(y_relay.at[zl, w], "y1", zl, w)
            y_send[zl, 2, w] = (y_part(zl, ymod(y + Y + step), w) + y_relay[zl, w].astype(f32)).astype(bf16)
            send(y_send.at[zl, 2, w], y_recv.at[zl, 0, w], ("y3", zl, w), side)

    fin = [(sem("fin", k), sem("fin", k + 2)) for k in (0, 1)]
    fin_out = [(sem("fout", k), sem("fout", k + 2)) for k in (0, 1)]
    assert fin[1][0] - fin[0][0] == 2

    def last(zl):
        device = {"z": x + X * zl, "x": home_x}
        return [
            pltpu.make_async_remote_copy(
                src_ref=src.at[zl], dst_ref=dst.at[half], send_sem=ssem.at[fin_out[zl][i]],
                recv_sem=rsem.at[fin[0][i] + 2 * half], device_id=device, device_id_type=MESH,
            )
            for i, (src, dst) in enumerate(((fin_send, fin_recv), (fina_send, fina_recv)))
        ]

    for zl in range(2):
        sums = []
        for w in range(2):
            arrived(y_recv.at[zl, 0, w], "y3", zl, w)
            arrived(y_recv.at[zl, 1, 1 - w], "y2", zl, 1 - w)
            sums.append(y_part(zl, y, w) + y_recv[zl, 0, w].astype(f32) + y_recv[zl, 1, 1 - w].astype(f32))
        total = jnp.concatenate(sums, axis=1)
        fin_send[zl] = total[0:ROWS].astype(bf16)
        fina_send[zl] = total[ROWS : ROWS + KEEP]
        elsewhere = jnp.logical_or(x + X * zl != z, home_x != x)

        @pl.when(elsewhere)
        def _():
            for c in last(zl):
                c.start()

        @pl.when(jnp.logical_not(elsewhere))
        def _():
            fin_recv[half] = fin_send[zl]
            fina_recv[half] = fina_send[zl]

    for h in range(2):
        @pl.when(jnp.logical_or(2 * x + h != z, lax.rem(z, X) != x))
        def _():
            for i, buffer in enumerate((fin_recv, fina_recv)):
                pltpu.make_async_remote_copy(
                    src_ref=buffer.at[h], dst_ref=buffer.at[h], send_sem=ssem.at[fin_out[0][i]],
                    recv_sem=rsem.at[fin[h][i]], device_id={"core": other}, device_id_type=MESH,
                ).wait_recv()

    out_m[:, 0:WIDE] = fin_recv[0].astype(f32)
    out_m[:, WIDE:] = fin_recv[1].astype(f32)[:, 2 * WIDE - BLOCK :]
    out_a[:, 0:WIDE] = fina_recv[0, 0:AROWS, :]
    out_a[:, WIDE:] = fina_recv[1, 0:AROWS, 2 * WIDE - BLOCK :]

    for c in sent:
        c.wait_send()
    for zl in range(2):

        @pl.when(jnp.logical_or(x + X * zl != z, home_x != x))
        def _():
            for c in last(zl):
                c.wait_send()

    assert len(names) <= 192


def local(mel, conv_weight, conv_bias, video_hidden, video_count, video_places, audio_places, cotangent):
    vmem = pl.BlockSpec(memory_space=pltpu.VMEM)
    hbm = pl.BlockSpec(memory_space=pl.ANY)
    part = (PART, WIDE)
    merger, audio = pl.pallas_call(
        kernel,
        out_shape=(
            jax.ShapeDtypeStruct((ROWS, BLOCK), f32),
            jax.ShapeDtypeStruct((AROWS, BLOCK), f32),
        ),
        in_specs=[vmem, vmem, vmem, hbm, vmem, vmem, vmem, hbm],
        out_specs=(vmem, vmem),
        scratch_shapes=[
            pltpu.VMEM((8, 128), i32),
            pltpu.VMEM((X, 8, 128), i32),
            pltpu.VMEM((X, Z, 8, 128), i32),
            pltpu.VMEM((X, Z, FRAMES, MELS), bf16),
            pltpu.VMEM((X, Z * SPOTS, WIDE), bf16),
            pltpu.VMEM((X, SLOTS, RROWS), bf16),
            pltpu.VMEM((Z, LIVE, RROWS), bf16),
            pltpu.VMEM((RROWS, Z * LIVE), bf16),
            pltpu.VMEM((X * Z * FRAMES, 4 * MELS), bf16),
            pltpu.VMEM((ENC, 4 * MELS), bf16),
            pltpu.VMEM((128, ENC), bf16),
            pltpu.VMEM((Z * LIVE, 128), i32),
            pltpu.VMEM((Z * LIVE, WIDE), f32),
            pltpu.VMEM((Z * LIVE, WIDE), bf16),
            pltpu.VMEM((RROWS, WIDE), f32),
            pltpu.VMEM((ENC, Z * SPOTS), bf16),
            pltpu.VMEM((ENC, WIDE), f32),
            pltpu.VMEM((3, 2, 2 * EROWS, HALF), bf16),
            pltpu.VMEM((2, 2 * EROWS, HALF), bf16),
            pltpu.VMEM((2, 2, 2 * EROWS, HALF), bf16),
            pltpu.VMEM((2, Y * C, APAD, WIDE), f32),
            pltpu.VMEM((2, Y, *part), f32),
            pltpu.VMEM((2, Y, *part), f32),
            pltpu.VMEM((2, Y, *part), f32),
            pltpu.VMEM((2, 3, 2, PART, HALF), bf16),
            pltpu.VMEM((2, 2, PART, HALF), bf16),
            pltpu.VMEM((2, 2, 2, PART, HALF), bf16),
            pltpu.VMEM((2, ROWS, WIDE), bf16),
            pltpu.VMEM((2, ROWS, WIDE), bf16),
            pltpu.VMEM((2, KEEP, WIDE), f32),
            pltpu.VMEM((2, KEEP, WIDE), f32),
            pltpu.VMEM((2, SLOTS, ZROWS), bf16),
            pltpu.VMEM((SPOTS // 2, WIDE), bf16),
            pltpu.SemaphoreType.DMA((192,)),
            pltpu.SemaphoreType.DMA((192,)),
        ],
        compiler_params=pltpu.CompilerParams(
            collective_id=0, has_side_effects=True, vmem_limit_bytes=60 * 2**20
        ),
    )(
        mel[0], conv_weight, conv_bias[None], video_hidden[0],
        video_count, video_places, audio_places, cotangent[0],
    )
    return merger[None], audio[None]


def solution(mesh):
    whole = Mesh(mesh.devices.reshape(Z, X, Y, C), ("z", "x", "y", "core"))
    dp, ctx = ("y", "core"), ("z", "x")
    return jax.shard_map(
        local,
        mesh=whole,
        in_specs=(
            P(dp, ctx, None),
            P(),
            P(),
            P(dp, ctx, None),
            P(dp, ctx),
            P(dp, ctx),
            P(dp, ctx),
            P(dp, ctx, None),
        ),
        out_specs=(P(ctx, dp, None), P(ctx, dp, None)),
        check_vma=False,
    )
```

time: 176 us -> 162 us (0.920); the launches traced: 174 us -> 162 us
  Pallas kernels: 168 us -> 156 us
    pallas_call x1, Pallas kernels: 168 us -> 156 us  [local(): pl.pallas_call(kernel, out_shape=(jax.ShapeDtypeStruct((ROWS, BLOCK), f32...]
where the time goes in v3:
time: 162 us
  Pallas kernels  156 us (96%)
  local copies, waits for them, and re-layouts  4.58 us (3%)
    pallas_call x1, Pallas kernels, local(): pl.pallas_call(kernel, out_shape=(jax.ShapeDtypeStruct((ROWS, BLOCK), f32...  156 us
    unnamed x2, local copies, waits for them, and re-layouts  3.28 us

profile of v3, /device:TPU:6, one launch (start us, length us, event | category | flops | bytes accessed | tf_op | source)
XLA Modules:
  0.0 161.7 jit_solution(6453653113953614156)
XLA Ops:
  1.3 1.3 broadcast_in_dim.9.bias
  2.6 155.9 %shard_map.95 = (f32[80,896]{1,0:T(8,128)}, f32[20,896]{1,0:T(8,128)}) custom-call(bf16[128,128]{1,0:T(8,128)(2,1)} %bitcast.9, bf16[384,1280]{1,0:T(8,128)(2,1)} %convw.1, f32[1,1280]{1,0:T(1,128)} %broadcast_in_dim.9.bias, bf16[128,5120]{1,0:T(8,128)(2,1)} %bitcast.6, s32[1,1]{1,0:T(1,128)S(6)} %copy.12.count, s32[1,128]{1,0:T(1,128)} %vplaces.1, ...), custom_call_target="tpu_custom_call" | custom-call | tf_op jit(solution)/shard_map/pallas_call | solution.py:538
  158.4 1.6 copy.10
  160.0 1.7 %copy.13 = f32[1,80,896]{2,1,0:T(8,128)} copy(f32[1,80,896]{2,1,0:T(8,128)} %bitcast.7) | data formatting | bytes 573440

commit v4 on v3

--- a/solution.py
+++ b/solution.py
@@ -326,47 +326,6 @@
             value = 128.0 * dot(pick, high, ((1,), (1,))) + dot(pick, rest, ((1,), (1,)))
             spot[pl.ds(pl.multiple_of(zs * LIVE + j * 128, 128), 128), :] = value.astype(i32)
 
-    ring(2)
-    b_in((3, 5))
-    forward((1, 7))
-    audio_piece(0)
-    arrived(b_half(zmod(z - 4), 0), "b", 4)
-    arrived(b_half(zmod(z + 4), 1), "b5")
-    b_out(4)
-    ring(3)
-    forward((2, 6))
-    audio_piece(1)
-    ring(4)
-    forward((3, 5))
-    audio_piece(2)
-    ring(5)
-    forward((4,))
-    audio_piece(3)
-
-    @pl.loop(0, ENC // 256)
-    def _(m):
-        at = pl.ds(pl.multiple_of(m * 256, 256), 256)
-        audio[at, :] = dot(acts[at, :], b_all[x])
-
-    def audio_rows(xt, w):
-        rows = [
-            audio[pl.ds(pl.multiple_of((xt + X * zl) * EROWS, 32), EROWS), w * HALF : (w + 1) * HALF]
-            for zl in range(2)
-        ]
-        return jnp.concatenate(rows, axis=0)
-
-    for w, (step, side) in enumerate(sides):
-        aud_send[0, w] = audio_rows(xmod(x + 2), w).astype(bf16)
-        send(aud_send.at[0, w], aud_relay.at[w], ("aud1", w), side)
-        aud_send[1, w] = audio_rows(xmod(x + step), 1 - w).astype(bf16)
-        send(aud_send.at[1, w], aud_recv.at[1, w], ("aud2", w), side)
-
-    def audio_relay():
-        for w, (step, side) in enumerate(sides):
-            arrived(aud_relay.at[w], "aud1", w)
-            aud_send[2, w] = (audio_rows(xmod(x + step), w) + aud_relay[w].astype(f32)).astype(bf16)
-            send(aud_send.at[2, w], aud_recv.at[0, w], ("aud3", w), side)
-
     lane = iota((256, 128), 1)
 
     def pick_rows(xs, part, first):
@@ -389,14 +348,69 @@
             else:
                 picked[at, :] += got
 
-    ring(6)
+    ring(2)
+    b_in((3, 5))
+    forward((1, 7))
+    audio_piece(0)
+    arrived(b_half(zmod(z - 4), 0), "b", 4)
+    arrived(b_half(zmod(z + 4), 1), "b5")
+    b_out(4)
+    forward((2, 6))
+    audio_piece(1)
+    ring(3)
+    forward((3,))
     pick_rows(x, 0, True)
+    audio_piece(2)
+    ring(4)
+    forward((5, 4))
+    audio_piece(3)
+
+    @pl.loop(0, ENC // 256)
+    def _(m):
+        at = pl.ds(pl.multiple_of(m * 256, 256), 256)
+        audio[at, :] = dot(acts[at, :], b_all[x])
+
+    def audio_rows(xt, w):
+        rows = [
+            audio[pl.ds(pl.multiple_of((xt + X * zl) * EROWS, 32), EROWS), w * HALF : (w + 1) * HALF]
+            for zl in range(2)
+        ]
+        return jnp.concatenate(rows, axis=0)
+
+    for w, (step, side) in enumerate(sides):
+        aud_send[0, w] = audio_rows(xmod(x + 2), w).astype(bf16)
+        send(aud_send.at[0, w], aud_relay.at[w], ("aud1", w), side)
+        aud_send[1, w] = audio_rows(xmod(x + step), 1 - w).astype(bf16)
+        send(aud_send.at[1, w], aud_recv.at[1, w], ("aud2", w), side)
+
+    def audio_relay():
+        for w, (step, side) in enumerate(sides):
+            arrived(aud_relay.at[w], "aud1", w)
+            aud_send[2, w] = (audio_rows(xmod(x + step), w) + aud_relay[w].astype(f32)).astype(bf16)
+            send(aud_send.at[2, w], aud_recv.at[0, w], ("aud3", w), side)
+
+    def turn(first, last):
+        @pl.loop(first, last)
+        def _(i):
+            zs = zmod(z + i)
+            for j in range(2):
+                a_t[:, pl.ds(pl.multiple_of(zs * LIVE + j * 128, 128), 128)] = a_all[
+                    zs, j * 128 : (j + 1) * 128, :
+                ].T
+
     pick_rows(x, 1, False)
-    audio_relay()
+    ring(5)
     pick_rows(xmod(x - 1), 0, False)
     pick_rows(xmod(x - 1), 1, False)
+    ring(6)
+    audio_relay()
     pick_rows(xmod(x + 1), 0, False)
     pick_rows(xmod(x + 1), 1, False)
+    turn(-2, 3)
+    for k in range(Z):
+        arrived(b_rows(xmod(x + 2), zmod(z - k)), "fr" if k < 4 else "fl", k)
+    pick_rows(xmod(x + 2), 0, False)
+    pick_rows(xmod(x + 2), 1, False)
 
     for t in range(3):
         for j in range(2):
@@ -406,18 +420,7 @@
                 arrived(a_rows(zmod(z + t + 1), j), "down", t, j)
     arrived(a_rows(zmod(z + 4), 0), "up", 3, 0)
     arrived(a_rows(zmod(z + 4), 1), "down", 3, 1)
-
-    @pl.loop(0, Z)
-    def _(zs):
-        for j in range(2):
-            a_t[:, pl.ds(pl.multiple_of(zs * LIVE + j * 128, 128), 128)] = a_all[
-                zs, j * 128 : (j + 1) * 128, :
-            ].T
-
-    for k in range(Z):
-        arrived(b_rows(xmod(x + 2), zmod(z - k)), "fr" if k < 4 else "fl", k)
-    pick_rows(xmod(x + 2), 0, False)
-    pick_rows(xmod(x + 2), 1, False)
+    turn(3, 6)
 
     aud_part[...] = jnp.zeros_like(aud_part)
     sums = []

time: 162 us -> 154 us (0.951)
  Pallas kernels: 156 us -> 148 us
    pallas_call x1, Pallas kernels: 156 us -> 148 us  [local(): pl.pallas_call(kernel, out_shape=(jax.ShapeDtypeStruct((ROWS, BLOCK), f32...]
where the time goes in v4:
time: 154 us
  Pallas kernels  148 us (96%)
  local copies, waits for them, and re-layouts  4.58 us (3%)
    pallas_call x1, Pallas kernels, local(): pl.pallas_call(kernel, out_shape=(jax.ShapeDtypeStruct((ROWS, BLOCK), f32...  148 us
    unnamed x2, local copies, waits for them, and re-layouts  3.28 us

profile of v4, /device:TPU:6, one launch (start us, length us, event | category | flops | bytes accessed | tf_op | source)
XLA Modules:
  0.0 153.8 jit_solution(12107981688228535767)
XLA Ops:
  1.3 1.3 broadcast_in_dim.9.bias
  2.6 147.9 %shard_map.95 = (f32[80,896]{1,0:T(8,128)}, f32[20,896]{1,0:T(8,128)}) custom-call(bf16[128,128]{1,0:T(8,128)(2,1)} %bitcast.9, bf16[384,1280]{1,0:T(8,128)(2,1)} %convw.1, f32[1,1280]{1,0:T(1,128)} %broadcast_in_dim.9.bias, bf16[128,5120]{1,0:T(8,128)(2,1)} %bitcast.6, s32[1,1]{1,0:T(1,128)S(6)} %copy.12.count, s32[1,128]{1,0:T(1,128)} %vplaces.1, ...), custom_call_target="tpu_custom_call" | custom-call | tf_op jit(solution)/shard_map/pallas_call | solution.py:541
  150.5 1.6 %copy.10 = f32[1,20,896]{2,0,1:T(1,128)} copy(f32[1,20,896]{2,1,0:T(8,128)} %bitcast.8) | data formatting | bytes 143360
  152.1 1.7 %copy.13 = f32[1,80,896]{2,1,0:T(8,128)} copy(f32[1,80,896]{2,1,0:T(8,128)} %bitcast.7) | data formatting | bytes 573440

commit v5 on v4

--- a/solution.py
+++ b/solution.py
@@ -328,22 +328,26 @@
 
     lane = iota((256, 128), 1)
 
-    def pick_rows(xs, part, first):
+    def pick_rows(xs, parts, first=False, last=False):
         span = 4 * SPOTS
+        blocks = pl.ds(parts[0] * span, len(parts) * span)
 
         @pl.loop(0, Z)
         def _(q):
             at = pl.ds(pl.multiple_of(q * LIVE, LIVE), LIVE)
             spots = spot[at, :]
             tiles = []
-            for t in range(span // 128):
-                ends = []
-                for s in (2 * t, 2 * t + 1):
-                    ends.append((4 * part + s // 3) * X * SPOTS + (s % 3) * 64)
-                there = jnp.where(lane < 64, lane + ends[0], lane - 64 + ends[1]) + xs * SPOTS
-                tiles.append(one_hot(spots == there))
-            got = dot(jnp.concatenate(tiles, axis=1), b_all[xs, part * span : (part + 1) * span, :])
-            if first:
+            for part in parts:
+                for t in range(span // 128):
+                    ends = []
+                    for s in (2 * t, 2 * t + 1):
+                        ends.append((4 * part + s // 3) * X * SPOTS + (s % 3) * 64)
+                    there = jnp.where(lane < 64, lane + ends[0], lane - 64 + ends[1]) + xs * SPOTS
+                    tiles.append(one_hot(spots == there))
+            got = dot(jnp.concatenate(tiles, axis=1), b_all[xs, blocks, :])
+            if last:
+                picked_b[at, :] = (picked[at, :] + got).astype(bf16)
+            elif first:
                 picked[at, :] = got
             else:
                 picked[at, :] += got
@@ -359,7 +363,7 @@
     audio_piece(1)
     ring(3)
     forward((3,))
-    pick_rows(x, 0, True)
+    pick_rows(x, (0,), first=True)
     audio_piece(2)
     ring(4)
     forward((5, 4))
@@ -398,19 +402,16 @@
                     zs, j * 128 : (j + 1) * 128, :
                 ].T
 
-    pick_rows(x, 1, False)
+    pick_rows(x, (1,))
     ring(5)
-    pick_rows(xmod(x - 1), 0, False)
-    pick_rows(xmod(x - 1), 1, False)
+    pick_rows(xmod(x - 1), (0, 1))
     ring(6)
     audio_relay()
-    pick_rows(xmod(x + 1), 0, False)
-    pick_rows(xmod(x + 1), 1, False)
+    pick_rows(xmod(x + 1), (0, 1))
     turn(-2, 3)
     for k in range(Z):
         arrived(b_rows(xmod(x + 2), zmod(z - k)), "fr" if k < 4 else "fl", k)
-    pick_rows(xmod(x + 2), 0, False)
-    pick_rows(xmod(x + 2), 1, False)
+    pick_rows(xmod(x + 2), (0, 1), last=True)
 
     for t in range(3):
         for j in range(2):
@@ -434,7 +435,6 @@
             at = zl * EROWS + d * AROWS
             aud_part[zl, d, 0:AROWS, :] = audio[at : at + AROWS, :]
 
-    picked_b[...] = picked[...].astype(bf16)
     other = 1 - core
 
     for zl in range(2):

time: 154 us -> 152 us (0.987)
  Pallas kernels: 148 us -> 145 us
    pallas_call x1, Pallas kernels: 148 us -> 145 us  [local(): pl.pallas_call(kernel, out_shape=(jax.ShapeDtypeStruct((ROWS, BLOCK), f32...]
where the time goes in v5:
time: 152 us; the launch traced here: 151 us
  Pallas kernels  145 us (95%)
  local copies, waits for them, and re-layouts  4.58 us (3%)
    pallas_call x1, Pallas kernels, local(): pl.pallas_call(kernel, out_shape=(jax.ShapeDtypeStruct((ROWS, BLOCK), f32...  145 us
    unnamed x2, local copies, waits for them, and re-layouts  3.28 us

profile of v5, /device:TPU:6, one launch (start us, length us, event | category | flops | bytes accessed | tf_op | source)
XLA Modules:
  0.0 151.0 jit_solution(5938333167721842324)
XLA Ops:
  1.3 1.3 broadcast_in_dim.9.bias
  2.6 145.2 %shard_map.95 = (f32[80,896]{1,0:T(8,128)}, f32[20,896]{1,0:T(8,128)}) custom-call(bf16[128,128]{1,0:T(8,128)(2,1)} %bitcast.9, bf16[384,1280]{1,0:T(8,128)(2,1)} %convw.1, f32[1,1280]{1,0:T(1,128)} %broadcast_in_dim.9.bias, bf16[128,5120]{1,0:T(8,128)(2,1)} %bitcast.6, s32[1,1]{1,0:T(1,128)S(6)} %copy.12.count, s32[1,128]{1,0:T(1,128)} %vplaces.1, ...), custom_call_target="tpu_custom_call" | custom-call | tf_op jit(solution)/shard_map/pallas_call | solution.py:541
  147.8 1.6 %copy.10 = f32[1,20,896]{2,0,1:T(1,128)} copy(f32[1,20,896]{2,1,0:T(8,128)} %bitcast.8) | data formatting | bytes 143360
  149.3 1.7 %copy.13 = f32[1,80,896]{2,1,0:T(8,128)} copy(f32[1,80,896]{2,1,0:T(8,128)} %bitcast.7) | data formatting | bytes 573440

commit v6 on v5

--- a/solution.py
+++ b/solution.py
@@ -10,6 +10,7 @@
 FRAMES, SLOTS, SPOTS = 128, 128, 192
 BLOCK = OUT // X
 WIDE = 512
+MAIN = 384
 RROWS = HID // X
 ROWS = HID // Z // (Y * C)
 AROWS = ENC // Z // (Y * C)
@@ -59,6 +60,8 @@
     home_x = lax.div(z, 2)
     half = lax.rem(z, 2)
 
+    b_all[x, :, MAIN:] = jnp.zeros((Z * SPOTS, WIDE - MAIN), bf16)
+
     barrier = pltpu.get_barrier_semaphore()
     peers = [{"z": zmod(z + k)} for k in range(1, Z)]
     peers += [{"x": xmod(x + k)} for k in range(1, X)]
@@ -98,14 +101,47 @@
     def arrived(dst, *key):
         copy(dst, dst, key, {"core": 1 - core}).wait_recv()
 
-    def window(zt):
-        return pl.ds(pl.multiple_of(lax.div(zt, 2) * BLOCK + lax.rem(zt, 2) * (BLOCK - WIDE), 128), WIDE)
+    main, rest = pl.ds(0, MAIN), pl.ds(MAIN, WIDE - MAIN)
+
+    def main_cols(zt):
+        return pl.ds(pl.multiple_of(lax.div(zt, 2) * BLOCK + lax.rem(zt, 2) * WIDE, 128), MAIN)
+
+    def rest_cols(zt):
+        return pl.ds(pl.multiple_of(lax.div(zt, 2) * BLOCK + MAIN, 128), WIDE - MAIN)
+
+    def even(zt):
+        return lax.rem(zt, 2) == 0
+
+    maybe = []
+
+    def send_wide(pieces, key, zt, device):
+        send(*pieces[0], key, device)
+
+        @pl.when(even(zt))
+        def _():
+            copy(*pieces[1], (*key, "rest"), device).start()
+
+        maybe.append((zt, lambda: copy(*pieces[1], (*key, "rest"), device)))
+
+    def arrived_wide(refs, zt, *key):
+        arrived(refs[0], *key)
+
+        @pl.when(even(zt))
+        def _():
+            arrived(refs[1], *key, "rest")
 
     def b_rows(xs, zs):
         return b_all.at[xs, pl.ds(pl.multiple_of(zs * SPOTS, 64), SPOTS)]
 
-    def b_half(zs, h):
-        return b_all.at[x, pl.ds(pl.multiple_of(zs * SPOTS + h * 96, 32), 96)]
+    def b_parts(zs, first=0, count=SPOTS):
+        rows = pl.ds(pl.multiple_of(zs * SPOTS + first, 32), count)
+        return b_all.at[x, rows, main], b_all.at[x, rows, rest]
+
+    def cot_parts(zt, first=0, count=SPOTS):
+        rows = pl.ds(first, count)
+        return cot.at[rows, main_cols(zt)], cot.at[rows, rest_cols(zt)]
+
+    relay_parts = b_relay.at[:, main], b_relay.at[:, rest]
 
     def a_cols(xt, w):
         return hidden.at[:, pl.ds(pl.multiple_of((xt + X * w) * ZROWS, 128), ZROWS)]
@@ -140,15 +176,18 @@
         c = pltpu.make_async_copy(a_cols(x, w), a_slot(x, w), ssem.at[sem("own_a", w)])
         c.start()
         own_a.append(c)
-    own_b = pltpu.make_async_copy(cot.at[:, window(z)], b_rows(x, z), ssem.at[sem("own_b")])
-    own_b.start()
+    own_b = []
+    for i, (src, dst) in enumerate(zip(cot_parts(z), b_parts(z))):
+        c = pltpu.make_async_copy(src, dst, ssem.at[sem("own_b", i)])
+        c.start()
+        own_b.append(c)
     zt = zmod(z + 4)
-    send(cot.at[pl.ds(96, 96), window(zt)], b_relay, ("b4",), {"z": zmod(z - 1)})
+    send_wide(list(zip(cot_parts(zt, 96, 96), relay_parts)), ("b4",), zt, {"z": zmod(z - 1)})
     for k in (1, 7, 2, 6, 3, 5):
         zt = zmod(z + k)
-        send(cot.at[:, window(zt)], b_rows(x, z), ("b", k), {"z": zt})
+        send_wide(list(zip(cot_parts(zt), b_parts(z))), ("b", k), zt, {"z": zt})
     zt = zmod(z + 4)
-    send(cot.at[pl.ds(0, 96), window(zt)], b_half(z, 0), ("b", 4), {"z": zt})
+    send_wide(list(zip(cot_parts(zt, 0, 96), b_parts(z, 0, 96))), ("b", 4), zt, {"z": zt})
 
     def b_out(k):
         block = b_rows(x, zmod(z - k))
@@ -187,7 +226,8 @@
     for w, (step, side) in enumerate(sides):
         arrived(a_relay.at[w], "a2", w)
         send(a_relay.at[w], a_slot(xmod(x - step), w), ("a3", w), side)
-    own_b.wait()
+    for c in own_b:
+        c.wait()
     b_out(0)
 
     b0 = bias[...]
@@ -267,17 +307,18 @@
 
     def b_in(ks):
         for k in ks:
-            arrived(b_rows(x, zmod(z - k)), "b", k)
+            arrived_wide(b_parts(zmod(z - k)), z, "b", k)
             b_out(k)
 
     for w, (step, side) in enumerate(sides):
         rows = mel_half(xmod(x - step), w)
         arrived(rows, "mxa", step, w)
         send(rows, rows, ("mxb", w), side)
-    arrived(b_relay, "b4")
-    send(b_relay, b_half(zmod(z + 1), 1), ("b5",), {"z": zmod(z - 3)})
+    zt = zmod(z - 3)
+    arrived_wide(relay_parts, zt, "b4")
+    send_wide(list(zip(relay_parts, b_parts(zmod(z + 1), 96, 96))), ("b5",), zt, {"z": zt})
     for k in (1, 7):
-        arrived(b_rows(x, zmod(z - k)), "b", k)
+        arrived_wide(b_parts(zmod(z - k)), z, "b", k)
         b_out(k)
 
     forward((0,))
@@ -356,12 +397,12 @@
     b_in((3, 5))
     forward((1, 7))
     audio_piece(0)
-    arrived(b_half(zmod(z - 4), 0), "b", 4)
-    arrived(b_half(zmod(z + 4), 1), "b5")
+    arrived_wide(b_parts(zmod(z + 4), 0, 96), z, "b", 4)
+    arrived_wide(b_parts(zmod(z + 4), 96, 96), z, "b5")
     b_out(4)
     forward((2, 6))
+    ring(3)
     audio_piece(1)
-    ring(3)
     forward((3,))
     pick_rows(x, (0,), first=True)
     audio_piece(2)
@@ -409,20 +450,6 @@
     audio_relay()
     pick_rows(xmod(x + 1), (0, 1))
     turn(-2, 3)
-    for k in range(Z):
-        arrived(b_rows(xmod(x + 2), zmod(z - k)), "fr" if k < 4 else "fl", k)
-    pick_rows(xmod(x + 2), (0, 1), last=True)
-
-    for t in range(3):
-        for j in range(2):
-            if (t + 1, j) not in up_items:
-                arrived(a_rows(zmod(z - t - 1), j), "up", t, j)
-            if (t + 1, j) not in down_items:
-                arrived(a_rows(zmod(z + t + 1), j), "down", t, j)
-    arrived(a_rows(zmod(z + 4), 0), "up", 3, 0)
-    arrived(a_rows(zmod(z + 4), 1), "down", 3, 1)
-    turn(3, 6)
-
     aud_part[...] = jnp.zeros_like(aud_part)
     sums = []
     for w in range(2):
@@ -434,6 +461,20 @@
         for d in range(Y * C):
             at = zl * EROWS + d * AROWS
             aud_part[zl, d, 0:AROWS, :] = audio[at : at + AROWS, :]
+
+    for k in range(Z):
+        arrived(b_rows(xmod(x + 2), zmod(z - k)), "fr" if k < 4 else "fl", k)
+    pick_rows(xmod(x + 2), (0, 1), last=True)
+
+    for t in range(3):
+        for j in range(2):
+            if (t + 1, j) not in up_items:
+                arrived(a_rows(zmod(z - t - 1), j), "up", t, j)
+            if (t + 1, j) not in down_items:
+                arrived(a_rows(zmod(z + t + 1), j), "down", t, j)
+    arrived(a_rows(zmod(z + 4), 0), "up", 3, 0)
+    arrived(a_rows(zmod(z + 4), 1), "down", 3, 1)
+    turn(3, 6)
 
     other = 1 - core
 
@@ -518,12 +559,18 @@
                 ).wait_recv()
 
     out_m[:, 0:WIDE] = fin_recv[0].astype(f32)
-    out_m[:, WIDE:] = fin_recv[1].astype(f32)[:, 2 * WIDE - BLOCK :]
+    out_m[:, WIDE:] = fin_recv[1].astype(f32)[:, 0:MAIN]
     out_a[:, 0:WIDE] = fina_recv[0, 0:AROWS, :]
-    out_a[:, WIDE:] = fina_recv[1, 0:AROWS, 2 * WIDE - BLOCK :]
+    out_a[:, WIDE:] = fina_recv[1, 0:AROWS, 0:MAIN]
 
     for c in sent:
         c.wait_send()
+    for zt, again in maybe:
+
+        @pl.when(even(zt))
+        def _():
+            again().wait_send()
+
     for zl in range(2):
 
         @pl.when(jnp.logical_or(x + X * zl != z, home_x != x))

time: 152 us -> 147 us (0.967)
  Pallas kernels: 145 us -> 140 us
    pallas_call x1, Pallas kernels: 145 us -> 140 us  [local(): pl.pallas_call(kernel, out_shape=(jax.ShapeDtypeStruct((ROWS, BLOCK), f32...]
where the time goes in v6:
time: 147 us; the launch traced here: 146 us
  Pallas kernels  140 us (95%)
  local copies, waits for them, and re-layouts  4.58 us (3%)
    pallas_call x1, Pallas kernels, local(): pl.pallas_call(kernel, out_shape=(jax.ShapeDtypeStruct((ROWS, BLOCK), f32...  140 us
    unnamed x2, local copies, waits for them, and re-layouts  3.28 us

profile of v6, /device:TPU:6, one launch (start us, length us, event | category | flops | bytes accessed | tf_op | source)
XLA Modules:
  0.0 145.9 jit_solution(6827297221625702600)
XLA Ops:
  1.3 1.3 broadcast_in_dim.9.bias
  2.6 140.0 %shard_map.95 = (f32[80,896]{1,0:T(8,128)}, f32[20,896]{1,0:T(8,128)}) custom-call(bf16[128,128]{1,0:T(8,128)(2,1)} %bitcast.9, bf16[384,1280]{1,0:T(8,128)(2,1)} %convw.1, f32[1,1280]{1,0:T(1,128)} %broadcast_in_dim.9.bias, bf16[128,5120]{1,0:T(8,128)(2,1)} %bitcast.6, s32[1,1]{1,0:T(1,128)S(6)} %copy.12.count, s32[1,128]{1,0:T(1,128)} %vplaces.1, ...), custom_call_target="tpu_custom_call" | custom-call | tf_op jit(solution)/shard_map/pallas_call | solution.py:588
  142.6 1.6 %copy.10 = f32[1,20,896]{2,0,1:T(1,128)} copy(f32[1,20,896]{2,1,0:T(8,128)} %bitcast.8) | data formatting | bytes 143360
  144.2 1.7 %copy.13 = f32[1,80,896]{2,1,0:T(8,128)} copy(f32[1,80,896]{2,1,0:T(8,128)} %bitcast.7) | data formatting | bytes 573440
